TPU v7x, 1024 devices: a whole 4x8x16 slice. The times are simulated.
1024 devices in a mesh: pipe: 8 (over y), ctx: 32 (over z, core), tp: 4 (over x).
Axes of the slice: x: 4, y: 8, z: 16, core: 2. Of those that a mesh axis runs over, the one named last changes fastest.
Arguments:
- queries: bfloat16 [8, 4096, 32, 128], P('pipe', 'ctx', 'tp'), may hold values from -45 to 45
- key_value: bfloat16 [8, 2, 4096, 8, 128], P('pipe', None, 'ctx', 'tp'), may hold values from -6 to 6
- mamba_in: bfloat16 [8, 4096, 8192], P('pipe', 'ctx', 'tp'), may hold values from -6 to 6
- gate_in: bfloat16 [8, 4096, 8192], P('pipe', 'ctx', 'tp'), may hold values from -6 to 6
- step_low: bfloat16 [8, 4096, 512], P('pipe', 'ctx'), may hold values from -3 to 3
- step_weight: bfloat16 [8, 512, 8192], P('pipe', None, 'tp'), may hold values from -0.25 to 0.25
- step_bias: float32 [8, 8192], P('pipe', 'tp'), may hold values from -4.6 to -3.2
- decay_rate: float32 [8, 8, 8192], P('pipe', None, 'tp'), may hold values from 0.0061035156 to 2.5
- conv_weight: float32 [8, 4, 8192], P('pipe', None, 'tp'), may hold values from -3 to 3
- conv_bias: float32 [8, 8192], P('pipe', 'tp'), may hold values from -3 to 3
- state_weight: bfloat16 [8, 8192, 16], P('pipe', 'tp'), may hold values from -0.0625 to 0.0625
- skip_gain: float32 [8, 8192], P('pipe', 'tp'), may hold values from 0.5 to 1.5
Outputs:
- attended: bfloat16 [8, 4096, 32, 128], P('pipe', 'ctx', 'tp')
- mamba_out: bfloat16 [8, 4096, 8192], P('pipe', 'ctx', 'tp')
All inputs are finite; a program needn't handle non-finite values.
Results may differ from a plain program's by a relative error of at most 0.023.
Values may be sent and summed in bfloat16 or wider, within the bound.
No kernel may reach another device: no remote copies, remote signals or barrier semaphores. Data moves between devices by JAX's collectives and lax.ppermute only.
A program may use at most 64 MiB of HBM per device.

v0:
```python
import math

import jax
import jax.numpy as jnp
from jax import lax
from jax.sharding import PartitionSpec as P


def passed_along(value, axis, steps):
    count = lax.axis_size(axis)
    leading, last = (max(0, -steps), min(count, count - steps))
    return lax.ppermute(value, axis, [(source, source + steps) for source in range(leading, last)])


def prefix(x, axis, join, neutral):
    place = lax.axis_index(axis)
    gathered = jax.tree.map(
        lambda a, kind: lax.all_gather(a.astype(kind), axis), x, (jnp.bfloat16, jnp.bfloat16)
    )
    state = jax.tree.map(lambda a, e: jnp.zeros_like(a) + jnp.asarray(e, a.dtype), x, neutral)

    def one(hop, state):
        return join(
            state,
            jax.tree.map(
                lambda a, own: lax.dynamic_index_in_dim(a, hop, 0, False).astype(own.dtype),
                gathered,
                x,
            ),
        )

    return lax.fori_loop(0, place, one, state)


def passed_along_2(block, axis, distance):
    devices = range(lax.axis_size(axis))
    route = [((i - distance) % len(devices), i) for i in devices]
    return lax.ppermute(block, axis, route)


def empty_state(kv_count, group_size, query_rows, head_width):
    return (
        jnp.full((kv_count, group_size, query_rows), -1e30, jnp.float32),
        jnp.zeros((kv_count, group_size, query_rows), jnp.float32),
        jnp.zeros((kv_count, group_size, query_rows, head_width), jnp.float32),
    )


def absorb(softmax_state, query_block, query_pos, kv_piece, key_pos):

    def compute(current):
        running_max, running_sum, weighted = current
        scores = jnp.einsum(
            "tkgd,skd->kgts", query_block, kv_piece[0], preferred_element_type=jnp.float32
        ) / math.sqrt(query_block.shape[-1])
        allowed = key_pos[None, :] <= query_pos[:, None]
        new_max = jnp.maximum(running_max, jnp.max(jnp.where(allowed, scores, -1e30), axis=-1))
        weights = jnp.where(allowed, jnp.exp(scores - new_max[..., None]), 0.0)
        running_sum = jnp.sum(weights, axis=-1)
        weighted = jnp.einsum(
            "kgts,skd->kgtd",
            weights.astype(jnp.bfloat16),
            kv_piece[1],
            preferred_element_type=jnp.float32,
        )
        return (new_max, running_sum, weighted)

    def unchanged(current):
        return current

    return lax.cond(key_pos[0] <= query_pos[-1], compute, unchanged, softmax_state)


def finish(softmax_state):
    weighted = softmax_state[2] / softmax_state[1][..., None]
    kv_count, group_size, query_rows, head_width = weighted.shape
    return (
        jnp.transpose(weighted, (2, 0, 1, 3))
        .reshape(query_rows, kv_count * group_size, head_width)
        .astype(jnp.bfloat16)
    )


def attend(queries, key_value):
    tok_rows, head_count, head_width = queries.shape
    kv_count = key_value.shape[2]
    group_size = head_count // kv_count
    ctx_index = lax.axis_index("ctx")
    half_rows = tok_rows // 2
    upper_query = queries[half_rows:]
    lower_pos = ctx_index * tok_rows + jnp.arange(half_rows, dtype=jnp.int32)
    upper_pos = ctx_index * tok_rows + half_rows + jnp.arange(tok_rows - half_rows, dtype=jnp.int32)
    lower_query = queries[:half_rows].reshape(half_rows, kv_count, group_size, head_width)
    upper_block = upper_query.reshape(tok_rows - half_rows, kv_count, group_size, head_width)
    initial = (
        empty_state(kv_count, group_size, half_rows, head_width),
        empty_state(kv_count, group_size, tok_rows - half_rows, head_width),
    )
    kv_piece = lax.all_gather(key_value, "ctx", axis=1, tiled=True)
    key_pos = jnp.arange(kv_piece.shape[1], dtype=jnp.int32)
    lower_out = finish(absorb(initial[0], lower_query, lower_pos, kv_piece, key_pos))
    upper_out = finish(absorb(initial[1], upper_block, upper_pos, kv_piece, key_pos))
    return jnp.concatenate([lower_out, upper_out], axis=0)


def mamba_layer(
    mamba_in,
    gate_in,
    step_low,
    step_weight,
    step_bias,
    decay_rate,
    conv_weight,
    conv_bias,
    state_weight,
    skip_gain,
):
    tok_rows, channels = mamba_in.shape
    state_count = decay_rate.shape[0]
    taps = conv_weight.shape[0]
    earlier_rows = passed_along(mamba_in[tok_rows - (taps - 1) :], "ctx", 1)
    padded = jnp.concatenate([earlier_rows, mamba_in], axis=0).astype(jnp.float32)
    conv_out = conv_bias[None, :]
    for tap_index in range(taps):
        conv_out = (
            conv_out + conv_weight[tap_index][None, :] * padded[tap_index : tap_index + tok_rows]
        )
    inner_act = jax.nn.silu(conv_out).astype(jnp.bfloat16)
    entry_read = lax.psum(
        jnp.dot(inner_act, state_weight, preferred_element_type=jnp.float32), "tp"
    )
    entry_map = entry_read[:, :state_count]
    read_map = entry_read[:, state_count:]
    step_size = jax.nn.softplus(
        jnp.dot(step_low, step_weight, preferred_element_type=jnp.float32) + step_bias[None, :]
    )
    drive_input = step_size * inner_act.astype(jnp.float32)
    block_len = min(16, tok_rows)
    block_total = tok_rows // block_len

    def run_block(carry_state, block_rows):
        step_rows, drive_rows, entry_rows, read_rows = block_rows
        outputs = []
        for offset in range(block_len):
            carry_state = (
                jnp.exp(-decay_rate * step_rows[offset][None, :]) * carry_state
                + entry_rows[offset][:, None] * drive_rows[offset][None, :]
            )
            outputs.append(jnp.sum(read_rows[offset][:, None] * carry_state, axis=0))
        return (carry_state, jnp.stack(outputs))

    def blocked(array):
        return array.reshape((block_total, block_len) + array.shape[1:])

    local_state, local_out = lax.scan(
        run_block,
        jnp.zeros((state_count, channels), jnp.float32),
        (blocked(step_size), blocked(drive_input), blocked(entry_map), blocked(read_map)),
    )
    elapsed = jnp.cumsum(step_size, axis=0)
    decay_total = jnp.exp(-decay_rate * elapsed[-1][None, :])

    def combine(earlier, later):
        return (earlier[0] * later[0], earlier[1] * later[0] + later[1])

    carried = prefix(
        (decay_total, local_state),
        "ctx",
        combine,
        (jnp.ones_like(decay_total), jnp.zeros_like(local_state)),
    )
    entering = carried[1]
    carried_in = jnp.sum(
        read_map[:, :, None] * jnp.exp(-decay_rate[None] * elapsed[:, None, :]) * entering[None],
        axis=1,
    )
    scan_out = (
        local_out.reshape(tok_rows, channels)
        + carried_in
        + skip_gain[None, :] * inner_act.astype(jnp.float32)
    )
    return (scan_out * jax.nn.silu(gate_in.astype(jnp.float32))).astype(jnp.bfloat16)


def per_device(
    queries,
    key_value,
    mamba_in,
    gate_in,
    step_low,
    step_weight,
    step_bias,
    decay_rate,
    conv_weight,
    conv_bias,
    state_weight,
    skip_gain,
):
    mixed = attend(queries[0], key_value[0])
    gated = mamba_layer(
        mamba_in[0],
        gate_in[0],
        step_low[0],
        step_weight[0],
        step_bias[0],
        decay_rate[0],
        conv_weight[0],
        conv_bias[0],
        state_weight[0],
        skip_gain[0],
    )
    arrived = passed_along_2((mixed, gated), "pipe", 1)
    return (arrived[0][None], arrived[1][None])


def solution(mesh):
    return jax.shard_map(
        per_device,
        mesh=mesh,
        in_specs=(
            P("pipe", "ctx", "tp", None),
            P("pipe", None, "ctx", "tp", None),
            P("pipe", "ctx", "tp"),
            P("pipe", "ctx", "tp"),
            P("pipe", "ctx", None),
            P("pipe", None, "tp"),
            P("pipe", "tp"),
            P("pipe", None, "tp"),
            P("pipe", None, "tp"),
            P("pipe", "tp"),
            P("pipe", "tp", None),
            P("pipe", "tp"),
        ),
        out_specs=(P("pipe", "ctx", "tp", None), P("pipe", "ctx", "tp")),
        check_vma=False,
    )
```

profile of v0, /device:TPU:1, one launch (start us, length us, event | category | flops | bytes accessed | tf_op | source)
XLA Modules:
  0.0 300.2 jit_solution(11108848274033073852)
XLA Ops:
  8.1 5.4 %collective-permute-start.1 = (bf16[3,2048]{1,0:T(4,128)(2,1)S(1)}, bf16[3,2048]{1,0:T(4,128)(2,1)S(1)}, u32[]{:S(2)}, u32[]{:S(2)}) collective-permute-start(bf16[3,2048]{1,0:T(4,128)(2,1)S(1)} %slice_bitcast_fusion), channel_id=1, source_target_pairs={{0,4},{4,8},{8,12},{12,16},{16,20},{20,24},{24,28},{28,32},{32,36}... | collective-permute-start | bytes 36872 | tf_op jit(solution)/shard_map/ppermute | solution.py:12
  14.5 9.7 %collective-permute-done.1 = bf16[3,2048]{1,0:T(4,128)(2,1)S(1)} collective-permute-done((bf16[3,2048]{1,0:T(4,128)(2,1)S(1)}, bf16[3,2048]{1,0:T(4,128)(2,1)S(1)}, u32[]{:S(2)}, u32[]{:S(2)}) %collective-permute-start.1) | collective-permute-done | bytes 12320 | tf_op jit(solution)/shard_map/ppermute | solution.py:12
  24.2 1.2 maximum_convert_fusion
  25.5 3.7 %convert_multiply_fusion.3 = (f32[128,2048]{1,0:T(8,128)}, bf16[128,2048]{1,0:T(8,128)(2,1)}, f32[128,2048]{1,0:T(8,128)S(1)}) fusion(f32[131,2048]{1,0:T(8,128)S(1)} %maximum_convert_fusion, f32[2048]{0:T(1024)S(1)} %bitcast.413, f32[2048]{0:T(1024)S(1)} %bitcast.414, f32[2048]{0:T(1024)S(1)} %bitcast.412, f32[2048]{0:T(1024)S(1)} %bitcast.411, ...), kind=kOutput, calls=%fused_computation.175 | convolution fusion | flops 274202624 | bytes 9093120 | tf_op jit(solution)/shard_map/dot_general | solution.py:135
  29.2 1.8 reduce_window_sum.11
  32.6 1.3 fusion.79
  33.9 6.1 %psum.7 = f32[128,16]{0,1:T(8,128)S(1)} all-reduce(f32[128,16]{0,1:T(8,128)S(1)} %fusion.79), channel_id=1, replica_groups=mesh['pipe'=8,'ctx'=32,'tp'=4] {'tp'}, use_global_device_ids=true, to_apply=%region_8.9 | all-reduce | flops 2048 | bytes 16384 | tf_op jit(solution)/shard_map/psum | solution.py:129
  41.5 67.7 %while.28 = (s32[]{:T(128)}, f32[8,2048]{1,0:T(8,128)S(1)}, f32[8,16,2048]{2,1,0:T(8,128)}, f32[8,16,2048]{2,1,0:T(8,128)S(1)}, f32[8,2048]{1,0:T(8,128)S(1)}, /...) while((s32[]{:T(128)}, f32[8,2048]{1,0:T(8,128)S(1)}, ...), condition=%wide.region_26.27_spmd.clone, body=%wide.region_9.26_spmd.clone.sunk | while | flops 2097170 | bytes 3084072 | solution.py:155
  41.5 1.7 fusion.87
  43.2 1.9 constant_dynamic-slice_fusion.65
  45.1 1.1 multiply_reduce_fusion.21
  49.7 1.7 fusion.87
  51.5 2.1 constant_dynamic-slice_fusion.65
  53.6 1.1 multiply_reduce_fusion.21
  58.2 1.7 fusion.87
  59.9 1.9 constant_dynamic-slice_fusion.65
  66.4 1.7 fusion.87
  68.2 2.1 constant_dynamic-slice_fusion.65
  70.3 1.1 multiply_reduce_fusion.21
  74.9 1.9 fusion.87
  76.9 1.9 constant_dynamic-slice_fusion.65
  78.8 1.1 multiply_reduce_fusion.21
  83.4 1.7 fusion.87
  85.1 2.1 constant_dynamic-slice_fusion.65
  87.3 1.1 multiply_reduce_fusion.21
  91.9 2.0 fusion.87
  93.9 1.9 constant_dynamic-slice_fusion.65
  95.8 1.1 multiply_reduce_fusion.21
  100.4 1.9 fusion.87
  102.3 2.2 constant_dynamic-slice_fusion.65
  104.5 1.1 multiply_reduce_fusion.21
  109.8 1.6 copy.30
  114.1 71.8 %all-gather.10.cloned.1.call-done = bf16[256,2048]{1,0:T(8,128)(2,1)} async-done(((bf16[8,2048]{1,0:T(8,128)(2,1)}), bf16[256,2048]{1,0:T(8,128)(2,1)}) %all-gather.10.cloned.1.call-update) | async-done | bytes 1048592 | tf_op jit(solution)/shard_map/all_gather | solution.py:18
  186.7 4.7 %multiply_reduce_fusion.16 = f32[128,2048]{1,0:T(8,128)S(1)} fusion(f32[8,2048]{1,0:T(8,128)S(1)} %get-tuple-element.179, f32[128,2048]{1,0:T(8,128)} %reduce_window_sum.11, f32[8,2048]{1,0:T(8,128)S(1)} %get-tuple-element.787, f32[128,8]{1,0:T(8,128)} %copy.43), kind=kLoop, calls=%fused_computation.168 | loop fusion | flops 8126464 | bytes 2232320 | tf_op jit(solution)/shard_map/reduce_sum | solution.py:173
  191.5 1.9 fusion.66
  193.4 3.1 %collective-permute-start.2 = (bf16[128,2048]{1,0:T(8,128)(2,1)S(1)}, bf16[128,2048]{1,0:T(8,128)(2,1)}, u32[]{:S(2)}, u32[]{:S(2)}) collective-permute-start(bf16[128,2048]{1,0:T(8,128)(2,1)S(1)} %fusion.66), channel_id=1, source_target_pairs={{896,0},{0,128},{128,256},{256,384},{384,512},{512,640},{640,768},... | collective-permute-start | bytes 1572872 | tf_op jit(solution)/shard_map/ppermute | solution.py:38
  196.5 67.1 %all-gather.8.cloned.1.call-done = bf16[1,2,4096,2,128]{4,2,3,1,0:T(8,128)(2,1)} async-done(((bf16[1,2,128,2,128]{4,2,3,1,0:T(8,128)(2,1)}), bf16[1,2,4096,2,128]{4,2,3,1,0:T(8,128)(2,1)}) %all-gather.8.cloned.1.call-update) | async-done | bytes 4194320 | tf_op jit(solution)/shard_map/all_gather | solution.py:99
  263.7 8.1 %conditional.3 = (f32[2,4,64]{2,1,0:T(4,128)S(1)}, f32[2,4,64,128]{3,2,1,0:T(8,128)S(1)}) conditional(s32[]{:T(128)} %bitcast.22, () %tuple.44, (s32[4096]{0:T(1024)S(1)}, s32[64]{0:T(128)S(1)}, bf16[2,4096,2,128]{3,1,2,0:T(8,128)(2,1)}, bf16[1,128,8,128]{3,2,1,0:T(8,128)(2,1)S(1)}) %tuple.234), branch_computations={%region_4.5_spmd, %region_5.8_spmd} | conditional | flops 1097072128 | bytes 48396588 | solution.py:71
  263.9 3.3 %fusion.15 = (f32[2,4,64]{2,1,0:T(4,128)S(1)}, f32[2,4096,64,4]{1,2,3,0:T(8,128)S(1)}) fusion(pred[64,4096]{1,0:T(8,128)(4,1)S(1)} %broadcast_compare_fusion.1, bf16[64,2,4,128]{3,0,2,1:T(8,128)(2,1)S(1)} %bitcast.406, bf16[2,4096,2,128]{3,1,2,0:T(8,128)(2,1)} %get-tuple-element.146), kind=kOutput, calls=%fused_computation.20 | convolution fusion | flops 543161856 | bytes 10881024 | tf_op jit(solution)/shard_map/cond/branch_1_fun/tkgd,skd->kgts/dot_general | solution.py:53
  267.3 2.3 fusion.19
  269.6 2.1 fusion.20
  272.0 8.0 %conditional.2 = (f32[2,4,64]{2,1,0:T(4,128)S(1)}, f32[2,4,64,128]{3,2,1,0:T(8,128)S(1)}) conditional(s32[]{:T(128)} %bitcast.18, () %tuple.42, (s32[4096]{0:T(1024)S(1)}, s32[64]{0:T(128)S(1)}, bf16[2,4096,2,128]{3,1,2,0:T(8,128)(2,1)}, bf16[1,128,8,128]{3,2,1,0:T(8,128)(2,1)S(1)}) %tuple.235), branch_computations={%region_0.0_spmd, %region_1.4_spmd} | conditional | flops 1097072128 | bytes 48396588 | solution.py:71
  272.3 3.3 %fusion = (f32[2,4,64]{2,1,0:T(4,128)S(1)}, f32[2,4096,64,4]{1,2,3,0:T(8,128)S(1)}) fusion(pred[64,4096]{1,0:T(8,128)(4,1)S(1)} %broadcast_compare_fusion, bf16[64,2,4,128]{3,0,2,1:T(8,128)(2,1)S(1)} %bitcast.407, bf16[2,4096,2,128]{3,1,2,0:T(8,128)(2,1)} %get-tuple-element.142), kind=kOutput, calls=%fused_computation.2 | convolution fusion | flops 543161856 | bytes 10881024 | tf_op jit(solution)/shard_map/cond/branch_1_fun/tkgd,skd->kgts/dot_general | solution.py:53
  275.7 2.3 fusion.4
  278.0 2.0 fusion.5
  280.3 2.9 collective-permute-start
  283.2 7.8 %collective-permute-done = bf16[128,8,128]{2,1,0:T(8,128)(2,1)S(1)} collective-permute-done((bf16[128,8,128]{2,1,0:T(8,128)(2,1)S(1)}, bf16[128,8,128]{2,1,0:T(8,128)(2,1)S(1)}, u32[]{:S(2)}, u32[]{:S(2)}) %collective-permute-start) | collective-permute-done | bytes 262176 | tf_op jit(solution)/shard_map/ppermute | solution.py:38
  291.8 1.9 copy.71
  (103 shorter events, 39.3 us)
Async XLA Ops:
  7.2 18.3 %copy-start = (bf16[1,512,2048]{2,1,0:T(8,128)(2,1)S(1)}, bf16[1,512,2048]{2,1,0:T(8,128)(2,1)}, u32[]{:S(2)}) copy-start(bf16[1,512,2048]{2,1,0:T(8,128)(2,1)} %param.25) | copy-start | bytes 6291460
  7.2 106.9 %all-gather.6.cloned.1.call-start = ((), (), s32[]{:S(2)}) async-start(), calls=%async_computation | async-start | bytes 1081344 | tf_op jit(solution)/shard_map/all_gather | solution.py:18
  8.1 16.1 %collective-permute-start.1 = (bf16[3,2048]{1,0:T(4,128)(2,1)S(1)}, bf16[3,2048]{1,0:T(4,128)(2,1)S(1)}, u32[]{:S(2)}, u32[]{:S(2)}) collective-permute-start(bf16[3,2048]{1,0:T(4,128)(2,1)S(1)} %slice_bitcast_fusion), channel_id=1, source_target_pairs={{0,4},{4,8},{8,12},{12,16},{16,20},{20,24},{24,28},{28,32},{32,36}... | collective-permute-start | bytes 36872 | tf_op jit(solution)/shard_map/ppermute | solution.py:12
  24.2 7.7 %copy-start.3 = (f32[1,8,2048]{2,1,0:T(8,128)S(1)}, f32[1,8,2048]{2,1,0:T(8,128)}, u32[]{:S(2)}) copy-start(f32[1,8,2048]{2,1,0:T(8,128)} %param.27) | copy-start | bytes 196612
  25.5 7.1 %copy-start.2 = (bf16[1,2048,16]{1,2,0:T(8,128)(2,1)S(1)}, bf16[1,2048,16]{1,2,0:T(8,128)(2,1)}, u32[]{:S(2)}) copy-start(bf16[1,2048,16]{1,2,0:T(8,128)(2,1)} %param.30) | copy-start | bytes 196612
  32.6 153.3 %all-gather.10.cloned.1.call-start = ((), (), s32[]{:S(2)}) async-start(), calls=%async_computation.2 | async-start | bytes 1081344 | tf_op jit(solution)/shard_map/all_gather | solution.py:18
  109.2 154.5 %copy-start.1 = (bf16[1,128,8,128]{3,2,1,0:T(8,128)(2,1)S(1)}, bf16[1,128,8,128]{3,2,1,0:T(8,128)(2,1)}, u32[]{:S(2)}) copy-start(bf16[1,128,8,128]{3,2,1,0:T(8,128)(2,1)} %param.20) | copy-start | bytes 786436
  109.8 153.9 %all-gather.8.cloned.1.call-start = ((), (), s32[]{:S(2)}) async-start(), calls=%async_computation.1 | async-start | bytes 4325376 | tf_op jit(solution)/shard_map/all_gather | solution.py:99
  193.4 89.8 %collective-permute-start.2 = (bf16[128,2048]{1,0:T(8,128)(2,1)S(1)}, bf16[128,2048]{1,0:T(8,128)(2,1)}, u32[]{:S(2)}, u32[]{:S(2)}) collective-permute-start(bf16[128,2048]{1,0:T(8,128)(2,1)S(1)} %fusion.66), channel_id=1, source_target_pairs={{896,0},{0,128},{128,256},{256,384},{384,512},{512,640},{640,768},... | collective-permute-start | bytes 1572872 | tf_op jit(solution)/shard_map/ppermute | solution.py:38
  263.9 5.7 %copy-start.4 = (bf16[2,4096,2,128]{3,1,2,0:T(8,128)(2,1)S(1)}, bf16[2,4096,2,128]{3,1,2,0:T(8,128)(2,1)}, u32[]{:S(2)}) copy-start(bf16[2,4096,2,128]{3,1,2,0:T(8,128)(2,1)} %get-tuple-element.146) | copy-start | bytes 12582916 | tf_op jit(solution)/shard_map/cond
  272.3 5.7 %copy-start.5 = (bf16[2,4096,2,128]{3,1,2,0:T(8,128)(2,1)S(1)}, bf16[2,4096,2,128]{3,1,2,0:T(8,128)(2,1)}, u32[]{:S(2)}) copy-start(bf16[2,4096,2,128]{3,1,2,0:T(8,128)(2,1)} %get-tuple-element.142) | copy-start | bytes 12582916 | tf_op jit(solution)/shard_map/cond
  280.3 10.8 %collective-permute-start = (bf16[128,8,128]{2,1,0:T(8,128)(2,1)S(1)}, bf16[128,8,128]{2,1,0:T(8,128)(2,1)S(1)}, u32[]{:S(2)}, u32[]{:S(2)}) collective-permute-start(bf16[128,8,128]{2,1,0:T(8,128)(2,1)S(1)} %pad_maximum_fusion), channel_id=1, source_target_pairs={{896,0},{0,128},{128,256},{256,384},{384,512},{512,640},{640,768},... | collective-permute-start | bytes 786440 | tf_op jit(solution)/shard_map/ppermute | solution.py:38
Sparse Core Ops, SparseCore 0:
  32.7 73.6 all-gather.5
  109.9 75.9 all-gather.9
  189.2 74.4 all-gather.7
where the time goes:
time: 304 us; the launch traced here: 300 us
  waiting for transfers between devices  157 us (52%)
  local copies, waits for them, and re-layouts  47.5 us (16%)
  other arithmetic  47 us (15%)
  matrix products  15.8 us (5%)
  between operations  15.3 us (5%)
  starting transfers between devices  11.5 us (4%)
  blocking collectives  6.13 us (2%)
    all_gather x2, waiting for transfers between devices, prefix(): lax.all_gather(a.astype(kind), axis)  71.8 us
    all_gather x1, waiting for transfers between devices, attend(): kv_piece = lax.all_gather(key_value, 'ctx', axis=1, tiled=True)  67.1 us
    reduce_sum x32, other arithmetic, run_block(): outputs.append(jnp.sum(read_rows[offset][:, None] * carry_state, axis=0))  29.8 us
    slice x8, local copies, waits for them, and re-layouts, run_block(): drive_rows[offset][None, :]  16 us
    mul x8, local copies, waits for them, and re-layouts, run_block(): entry_rows[offset][:, None] * drive_rows[offset][None, :]  14.4 us
    ppermute x1, waiting for transfers between devices, passed_along(): lax.ppermute(value, axis, [(source, source + steps) for source in range(l...  9.74 us
    ppermute x2, waiting for transfers between devices, passed_along_2(): return lax.ppermute(block, axis, route)  7.85 us
    dot_general x2, matrix products, compute(): jnp.einsum('tkgd,skd->kgts', query_block, kv_piece[0], preferred_element_...  6.7 us
  transfers between devices with their start and end apart: 6, of which 4 were waited for; matrix products, arithmetic and copies ran while one was open for 33% of the time, Pallas kernels for 0%

commit v1 on v0

v1 whole, which is shorter than its diff:
```python
import functools
import math

import jax
import jax.numpy as jnp
from jax import lax
from jax.experimental import pallas as pl
from jax.experimental.pallas import tpu as pltpu
from jax.sharding import Mesh, PartitionSpec as P

LOG2E = math.log2(math.e)
CTX = ("zh", "zc", "core")
HALO = 16
F32 = jnp.float32
BF16 = jnp.bfloat16
VMEM = pl.BlockSpec(memory_space=pltpu.VMEM)
SMEM = pl.BlockSpec(memory_space=pltpu.SMEM)


def kernel_call(body, out_shape, args, specs=None, scratch=(), flops=0, nbytes=0, limit=48):
    outs = out_shape if isinstance(out_shape, (tuple, list)) else (out_shape,)
    return pl.pallas_call(
        body,
        out_shape=out_shape,
        in_specs=specs or [VMEM] * len(args),
        out_specs=jax.tree.map(lambda _: VMEM, out_shape),
        scratch_shapes=list(scratch),
        compiler_params=pltpu.CompilerParams(vmem_limit_bytes=limit << 20),
        cost_estimate=pl.CostEstimate(flops=flops, bytes_accessed=nbytes, transcendentals=0),
    )(*args)


def step_body(low_ref, weight_ref, bias_ref, step_ref):
    cols = weight_ref.shape[1]
    width = 512
    for at in range(0, cols, width):
        v = jnp.dot(low_ref[...], weight_ref[:, at : at + width], preferred_element_type=F32)
        v = v + bias_ref[:, at : at + width]
        step_ref[:, at : at + width] = jnp.maximum(v, 0.0) + jnp.log1p(jnp.exp(-jnp.abs(v)))


def conv_body(x_ref, halo_ref, weight_ref, bias_ref, proj_ref, act_ref, read_ref):
    rows, cols = x_ref.shape
    taps = weight_ref.shape[0]
    width = 256
    total = jnp.zeros(read_ref.shape, F32)
    for at in range(0, cols, width):
        lanes = slice(at, at + width)
        padded = jnp.concatenate([halo_ref[:, lanes].astype(F32), x_ref[:, lanes].astype(F32)], axis=0)
        v = bias_ref[:, lanes]
        for tap in range(taps):
            first = HALO - (taps - 1) + tap
            v = v + weight_ref[tap : tap + 1, lanes] * padded[first : first + rows]
        act = (v / (1.0 + jnp.exp(-v))).astype(BF16)
        act_ref[:, lanes] = act
        total = total + lax.dot_general(
            act, proj_ref[:, lanes], (((1,), (1,)), ((), ())), preferred_element_type=F32
        )
    read_ref[...] = total


def wide(row, count):
    return jnp.broadcast_to(row, (count, row.shape[1]))


def local_body(step_ref, act_ref, entry_ref, rate_ref, out_ref, drive_ref):
    rows, cols = step_ref.shape
    count = rate_ref.shape[0]
    drive_ref[...] = step_ref[...] * act_ref[...].astype(F32)
    rate = rate_ref[...] * -LOG2E

    def block(at, carry):
        state, elapsed = carry
        base = pl.multiple_of(at * 16, 16)
        for i in range(16):
            step = wide(step_ref[pl.ds(base + i, 1), :], count)
            drive = wide(drive_ref[pl.ds(base + i, 1), :], count)
            entry = jnp.concatenate([entry_ref[base + i]] * (cols // 128), axis=1)
            state = jnp.exp2(rate * step) * state + entry * drive
            elapsed = elapsed + step
        return state, elapsed

    zero = jnp.zeros((count, cols), F32)
    state, elapsed = lax.fori_loop(0, rows // 16, block, (zero, zero))
    decay = jnp.exp2(rate * elapsed)
    half = count // 2
    for part in range(2 * cols // 128):
        lanes = slice(part // 2 * 128, part // 2 * 128 + 128)
        top = part % 2 * half
        both = jnp.concatenate([state[top : top + half, lanes], decay[top : top + half, lanes]], axis=0)
        out_ref[part] = both.astype(out_ref.dtype)


def prefix_body(in_ref, after_ref, out_ref):
    places, both, lanes = in_ref.shape
    half = both // 2
    state = jnp.zeros((half, lanes), F32)
    for place in range(places):
        out_ref[place] = state
        pair = in_ref[place].astype(F32)
        state = pair[half:] * state + pair[:half]


def scan_body(step_ref, act_ref, entry_ref, read_ref, rate_ref, enter_ref, skip_ref, gate_ref, after_ref, out_ref, drive_ref, held_ref):
    rows, cols = step_ref.shape
    count = rate_ref.shape[0]
    span = held_ref.shape[0] // count
    drive_ref[...] = step_ref[...] * act_ref[...].astype(F32)
    rate = rate_ref[...] * -LOG2E
    wanted = lax.broadcasted_iota(jnp.int32, (2 * count, span * count), 1) % count + count
    spread = (lax.broadcasted_iota(jnp.int32, wanted.shape, 0) == wanted).astype(BF16)
    held_at = lax.broadcasted_iota(jnp.int32, (span, span * count), 1) // count
    own = held_at == lax.broadcasted_iota(jnp.int32, held_at.shape, 0)
    state = jnp.concatenate(
        [
            jnp.concatenate([enter_ref[2 * block], enter_ref[2 * block + 1]], axis=0)
            for block in range(cols // 128)
        ],
        axis=1,
    )

    def chunk(at, state):
        base = pl.multiple_of(at * span, span)
        for i in range(0, span, 2):
            pair = []
            for j in (i, i + 1):
                step = wide(step_ref[pl.ds(base + j, 1), :], count)
                drive = wide(drive_ref[pl.ds(base + j, 1), :], count)
                entry = jnp.concatenate([entry_ref[base + j]] * (cols // 128), axis=1)
                state = jnp.exp2(rate * step) * state + entry * drive
                pair.append(state)
            held_ref[i * count : (i + 2) * count, :] = jnp.concatenate(pair, axis=0).astype(BF16)
        read = jnp.dot(read_ref[pl.ds(base, span), :].astype(BF16), spread, preferred_element_type=F32)
        read = jnp.where(own, read, 0.0).astype(BF16)
        width = 512
        for lane in range(0, cols, width):
            lanes = slice(lane, lane + width)
            scanned = jnp.dot(read, held_ref[:, lanes], preferred_element_type=F32)
            act = act_ref[pl.ds(base, span), lanes].astype(F32)
            gate = gate_ref[pl.ds(base, span), lanes].astype(F32)
            full = scanned + skip_ref[:, lanes] * act
            out_ref[pl.ds(base, span), lanes] = (full * (gate / (1.0 + jnp.exp(-gate)))).astype(out_ref.dtype)
        return state

    lax.fori_loop(0, rows // span, chunk, state)


def attend_body(place_ref, q_ref, kv_ref, after_ref, out_ref, held_ref, top_ref, acc_ref, *, slot, group):
    cores, slots, _, rows, width = kv_ref.shape[1:]
    zh, zc, core = place_ref[0], place_ref[1], place_ref[2]
    keys = cores * slots * rows
    scale = LOG2E / math.sqrt(width)
    tile = 128
    tiles = [slice(first, first + tile) for first in range(0, q_ref.shape[0], tile)]
    query_block = 2 * (zc ^ slot) + core

    def scores_of(at, lines):
        k = kv_ref[at, :, :, 0].reshape(keys, width)
        return lax.dot_general(q_ref[lines, :], k, (((1,), (1,)), ((), ())), preferred_element_type=F32)

    def folded(s):
        return functools.reduce(jnp.maximum, [s[:, lane : lane + width] for lane in range(0, keys, width)])

    for lines in tiles:
        s = scores_of(zh, lines)
        line = lax.broadcasted_iota(jnp.int32, s.shape, 0) + lines.start
        column = lax.broadcasted_iota(jnp.int32, s.shape, 1)
        query_pos = query_block * rows + line // group
        key_block = 2 * (zc ^ (column // rows % slots)) + column // (rows * slots)
        s = jnp.where(key_block * rows + column % rows <= query_pos, s, -jnp.inf)
        held_ref[zh, lines, :] = s
        top_ref[lines, :] = folded(s)

    def score(at, _):
        for lines in tiles:
            s = scores_of(at, lines)
            held_ref[at, lines, :] = s
            top_ref[lines, :] = jnp.maximum(top_ref[lines, :], folded(s))
        return 0

    lax.fori_loop(0, zh, score, 0)
    for lines in tiles:
        top = jnp.max(top_ref[lines, :], axis=1, keepdims=True) * scale
        top_ref[lines, :] = jnp.broadcast_to(top, (tile, width))
    acc_ref[...] = jnp.zeros_like(acc_ref)
    ones = jnp.ones((keys, width), BF16)

    def weigh(at, _):
        v = jnp.concatenate([kv_ref[at, :, :, 1].reshape(keys, width), ones], axis=1)
        for lines in tiles:
            s, top = held_ref[at, lines, :], top_ref[lines, :]
            p = jnp.concatenate(
                [jnp.exp2(s[:, lane : lane + width] * scale - top).astype(BF16) for lane in range(0, keys, width)],
                axis=1,
            )
            acc_ref[lines, :] += jnp.dot(p, v, preferred_element_type=F32)
        return 0

    lax.fori_loop(0, zh + 1, weigh, 0)
    out_ref[...] = (acc_ref[:, :width] / acc_ref[:, width:]).astype(out_ref.dtype)


def per_device(
    queries,
    key_value,
    mamba_in,
    gate_in,
    step_low,
    step_weight,
    step_bias,
    decay_rate,
    conv_weight,
    conv_bias,
    state_weight,
    skip_gain,
):
    queries, key_value, mamba_in, gate_in = queries[0], key_value[0], mamba_in[0], gate_in[0]
    decay_rate, state_weight = decay_rate[0], state_weight[0]
    rows, heads, width = queries.shape
    kv_heads = key_value.shape[2]
    group = heads // kv_heads
    cols = mamba_in.shape[1]
    count = decay_rate.shape[0]
    taps = conv_weight.shape[1]
    pipes = lax.axis_size("pipe")
    places = lax.axis_size(CTX)
    zh, zc, core = (lax.axis_index(a) for a in CTX)
    swap = [(0, 1), (1, 0)]

    own_kv = lax.dynamic_index_in_dim(key_value, zc, 2, False)
    other_kv = lax.ppermute(lax.dynamic_index_in_dim(key_value, 1 - zc, 2, False), "zc", swap)
    halo = lax.ppermute(mamba_in[rows - HALO :], CTX, [(i, i + 1) for i in range(places - 1)])
    own_kv, other_kv, halo = lax.optimization_barrier((own_kv, other_kv, halo))
    kv = lax.all_gather(jnp.stack([own_kv, other_kv]), ("zh", "core"))
    kv = kv.reshape((lax.axis_size("zh"), lax.axis_size("core")) + kv.shape[1:])

    step = kernel_call(
        step_body,
        jax.ShapeDtypeStruct((rows, cols), F32),
        (step_low[0], step_weight[0], step_bias),
        flops=2 * rows * cols * step_low.shape[2],
        nbytes=4 << 20,
    )
    act, partial = kernel_call(
        conv_body,
        (jax.ShapeDtypeStruct((rows, cols), BF16), jax.ShapeDtypeStruct((rows, 2 * count), F32)),
        (mamba_in, halo, conv_weight[0], conv_bias, state_weight.T),
        nbytes=4 << 20,
    )
    entry_read = lax.psum(partial, "tp")
    queries, entry_read = lax.optimization_barrier((queries, entry_read))
    grouped = queries.reshape(rows, kv_heads, group, width)
    own_q = lax.dynamic_index_in_dim(grouped, zc, 1, False)
    other_q = lax.ppermute(lax.dynamic_index_in_dim(grouped, 1 - zc, 1, False), "zc", swap)
    place = jnp.stack([zh, zc, core]).astype(jnp.int32)

    entry = jnp.broadcast_to(entry_read[:, :count, None], (rows, count, 128))
    span = 32
    parts = kernel_call(
        local_body,
        jax.ShapeDtypeStruct((2 * cols // 128, count, 128), BF16),
        (step, act, entry, decay_rate),
        scratch=[pltpu.VMEM((rows, cols), F32)],
        nbytes=16 << 20,
    )
    parts = lax.all_to_all(parts, CTX, 0, 0, tiled=True)
    entering = kernel_call(
        prefix_body, jax.ShapeDtypeStruct((places, count // 2, 128), F32), (parts, other_q), nbytes=1 << 20
    )
    entering = lax.all_to_all(entering, CTX, 0, 0, tiled=True)
    def attend(q, slot, after):
        lines = rows * group
        keys = 4 * rows
        return kernel_call(
            functools.partial(attend_body, slot=slot, group=group),
            jax.ShapeDtypeStruct((lines, width), BF16),
            (place, q.reshape(lines, width), kv, after),
            specs=[SMEM, VMEM, VMEM, SMEM if after is place else VMEM],
            scratch=[
                pltpu.VMEM((places // 4, lines, keys), F32),
                pltpu.VMEM((lines, width), F32),
                pltpu.VMEM((lines, 2 * width), F32),
            ],
            flops=4 * lines * width * rows * places,
            nbytes=16 << 20,
        ).reshape(rows, group, width)

    far = attend(other_q, 1, place)
    far_sent = lax.ppermute(
        far,
        ("pipe", "zc"),
        [(2 * i + j, 2 * ((i + 1) % pipes) + 1 - j) for i in range(pipes) for j in range(2)],
    )
    gated = kernel_call(
        scan_body,
        jax.ShapeDtypeStruct((rows, cols), BF16),
        (step, act, entry, entry_read, decay_rate, entering, skip_gain, gate_in, far),

        scratch=[pltpu.VMEM((rows, cols), F32), pltpu.VMEM((span * count, cols), BF16)],
        nbytes=16 << 20,
    )
    mamba_out = lax.ppermute(gated, "pipe", [(i, (i + 1) % pipes) for i in range(pipes)])
    near = attend(own_q, 0, far_sent)
    near = lax.ppermute(near, "pipe", [(i, (i + 1) % pipes) for i in range(pipes)])
    far = far_sent
    first = jnp.where(zc == 0, near, far)
    second = jnp.where(zc == 0, far, near)
    attended = jnp.concatenate([first, second], axis=1)
    return (attended[None], mamba_out[None])


def solution(mesh):
    pipes, places, parts = mesh.devices.shape
    split = Mesh(
        mesh.devices.reshape(pipes, places // 4, 2, 2, parts), ("pipe", "zh", "zc", "core", "tp")
    )
    return jax.shard_map(
        per_device,
        mesh=split,
        in_specs=(
            P("pipe", CTX, "tp", None),
            P("pipe", None, CTX, "tp", None),
            P("pipe", CTX, "tp"),
            P("pipe", CTX, "tp"),
            P("pipe", CTX, None),
            P("pipe", None, "tp"),
            P("pipe", "tp"),
            P("pipe", None, "tp"),
            P("pipe", None, "tp"),
            P("pipe", "tp"),
            P("pipe", "tp", None),
            P("pipe", "tp"),
        ),
        out_specs=(P("pipe", CTX, "tp", None), P("pipe", CTX, "tp")),
        check_vma=False,
    )
```

time: 304 us -> 137 us (0.45)
  waiting for transfers between devices: 157 us -> 31.4 us
  other arithmetic: 47 us -> 1.61 us
  starting transfers between devices: 11.5 us -> 53.3 us
  local copies, waits for them, and re-layouts: 47.5 us -> 9.6 us
  matrix products: 15.8 us -> 0 us
  Pallas kernels: 0 us -> 14 us
  blocking collectives: 6.13 us -> 11.4 us
    all_gather x3 -> x1, waiting for transfers between devices: 139 us -> 0.01 us  [per_device(): kv = lax.all_gather(jnp.stack([own_kv, other_kv]), ('zh', 'core'))]
    reduce_sum x35 -> x0, other arithmetic: 39.2 us -> none  [the longest x32 29.8 us: run_block(): outputs.append(jnp.sum(read_rows[offset][:, None] * carry_state, axis=0))]
    all_to_all x0 -> x2, starting transfers between devices: none -> 29.7 us  [the longest x1 20.1 us: per_device(): parts = lax.all_to_all(parts, CTX, 0, 0, tiled=True)]
    slice x17 -> x1, local copies, waits for them, and re-layouts: 20 us -> 0.85 us  [per_device(): mamba_in[rows - HALO:]]
    dot_general x6 -> x0, matrix products: 15.8 us -> none  [the longest x2 6.7 us: compute(): jnp.einsum('tkgd,skd->kgts', query_block, kv_piece[0], preferred_element_...]
    mul x8 -> x0, local copies, waits for them, and re-layouts: 14.4 us -> none  [run_block(): entry_rows[offset][:, None] * drive_rows[offset][None, :]]
    pallas_call x0 -> x7, Pallas kernels: none -> 14 us  [kernel_call(): pl.pallas_call(body, out_shape=out_shape, in_specs=specs or [VMEM] * len(...]
    ppermute x3 -> x6, starting transfers between devices: 11.4 us -> 23.6 us  [the longest x1 5.38 us: per_device(): lax.ppermute(mamba_in[rows - HALO:], CTX, [(i, i + 1) for i in range(plac...]
  transfers between devices with their start and end apart: 6 -> 9, of which waited for: 4 -> 5; matrix products, arithmetic and copies ran while one was open for 33% -> 2% of each run, Pallas kernels for 0% -> 10%
where the time goes in v1:
time: 137 us; the launch traced here: 136 us
  starting transfers between devices  53.3 us (39%)
  waiting for transfers between devices  31.4 us (23%)
  between operations  14.3 us (10%)
  Pallas kernels  14 us (10%)
  blocking collectives  11.4 us (8%)
  local copies, waits for them, and re-layouts  9.6 us (7%)
  other arithmetic  1.61 us (1%)
    all_to_all x1, starting transfers between devices, per_device(): parts = lax.all_to_all(parts, CTX, 0, 0, tiled=True)  20.1 us
    pallas_call x7, Pallas kernels, kernel_call(): pl.pallas_call(body, out_shape=out_shape, in_specs=specs or [VMEM] * len(...  14 us
    psum x1, blocking collectives, per_device(): entry_read = lax.psum(partial, 'tp')  11.4 us
    ppermute x1, waiting for transfers between devices, per_device(): lax.ppermute(lax.dynamic_index_in_dim(grouped, 1 - zc, 1, False), 'zc', s...  10.4 us
    ppermute x1, waiting for transfers between devices, per_device(): lax.ppermute(near, 'pipe', [(i, (i + 1) % pipes) for i in range(pipes)])  9.84 us
    all_to_all x1, starting transfers between devices, per_device(): entering = lax.all_to_all(entering, CTX, 0, 0, tiled=True)  9.56 us
    unnamed x31, local copies, waits for them, and re-layouts  6.54 us
    ppermute x1, starting transfers between devices, per_device(): lax.ppermute(mamba_in[rows - HALO:], CTX, [(i, i + 1) for i in range(plac...  5.38 us
  transfers between devices with their start and end apart: 9, of which 5 were waited for; matrix products, arithmetic and copies ran while one was open for 2% of the time, Pallas kernels for 10%

profile of v1, /device:TPU:1, one launch (start us, length us, event | category | flops | bytes accessed | tf_op | source)
XLA Modules:
  0.0 135.6 jit_solution(9951307026061415801)
XLA Ops:
  7.2 0.0 all-gather.3.cloned.1.call-start
  7.2 0.8 slice_bitcast_fusion
  8.1 5.4 %collective-permute-start.1 = (bf16[16,2048]{1,0:T(8,128)(2,1)S(1)}, bf16[16,2048]{1,0:T(8,128)(2,1)S(1)}, u32[]{:S(2)}, u32[]{:S(2)}) collective-permute-start(bf16[16,2048]{1,0:T(8,128)(2,1)S(1)} %slice_bitcast_fusion), channel_id=1, source_target_pairs={{0,4},{4,8},{8,12},{12,16},{16,20},{20,24},{24,28},{28,32},{32,36}... | collective-permute-start | bytes 196616 | tf_op jit(solution)/shard_map/ppermute | solution.py:232
  13.4 1.3 constant_dynamic-slice_fusion.1
  14.7 0.0 copy-start.1
  14.7 0.0 copy-start.6
  14.7 0.0 copy-start.7
  14.7 0.0 copy-start.9
  14.8 4.1 %collective-permute-start = (bf16[2,128,128]{2,1,0:T(8,128)(2,1)S(1)}, bf16[2,128,128]{2,1,0:T(8,128)(2,1)S(1)}, u32[]{:S(2)}, u32[]{:S(2)}) collective-permute-start(bf16[2,128,128]{2,1,0:T(8,128)(2,1)S(1)} %bitcast.64), channel_id=1, source_target_pairs={{0,8},{8,0},{1,9},{9,1},{2,10},{10,2},{3,11},{11,3},{4,12},{12,4},... | collective-permute-start | bytes 196616 | tf_op jit(solution)/shard_map/ppermute | solution.py:231
  18.9 5.3 %collective-permute-done.1.halo_ref = bf16[16,2048]{1,0:T(8,128)(2,1)S(1)} collective-permute-done((bf16[16,2048]{1,0:T(8,128)(2,1)S(1)}, bf16[16,2048]{1,0:T(8,128)(2,1)S(1)}, u32[]{:S(2)}, u32[]{:S(2)}) %collective-permute-start.1) | collective-permute-done | bytes 65568 | tf_op jit(solution)/shard_map/ppermute | solution.py:232
  24.2 0.0 collective-permute-done
  24.2 0.7 pad_maximum_fusion
  24.9 0.0 all-gather.3.cloned.1.call-update
  24.9 0.0 copy-start
  24.9 1.6 %copy-done = bf16[1,512,2048]{2,1,0:T(8,128)(2,1)S(1)} copy-done((bf16[1,512,2048]{2,1,0:T(8,128)(2,1)S(1)}, bf16[1,512,2048]{2,1,0:T(8,128)(2,1)}, u32[]{:S(2)}) %copy-start) | copy-done | bytes 2097176
  26.5 0.9 copy-done.4
  27.4 0.7 copy-done.8
  28.1 0.8 shard_map.134.step_ref
  29.0 0.0 copy-start.13
  29.0 0.0 copy-done.1
  29.0 0.0 copy-done.6
  29.0 1.2 shard_map.131
  30.2 11.4 %psum.7.read_ref = f32[128,16]{1,0:T(8,128)S(1)} all-reduce(f32[128,16]{1,0:T(8,128)S(1)} %get-tuple-element.10), channel_id=1, replica_groups=mesh['pipe'=8,'zh'=8,'zc'=2,'core'=2,'tp'=4] {'tp'}, use_global_device_ids=true, to_apply=%region_0.1 | all-reduce | flops 2048 | bytes 16384 | tf_op jit(solution)/shard_map/psum | solution.py:250
  41.6 0.2 broadcast_in_dim.13.entry_ref
  41.8 3.7 %shard_map.135 = bf16[32,8,128]{2,1,0:T(8,128)(2,1)} custom-call(f32[128,2048]{1,0:T(8,128)S(1)} %shard_map.134.step_ref, bf16[128,2048]{1,0:T(8,128)(2,1)S(1)} %get-tuple-element.14.act_ref, f32[128,8,128]{2,1,0:T(8,128)S(1)} %broadcast_in_dim.13.entry_ref, f32[8,2048]{1,0:T(8,128)S(1)} %bitcast.47), custom_call_target="tpu_custom_call" | custom-call | bytes 16777216 | tf_op jit(solution)/shard_map/pallas_call | solution.py:22
  45.5 20.1 %all-to-all-start = ((bf16[32,8,128]{2,1,0:T(8,128)(2,1)}), bf16[32,8,128]{2,1,0:T(8,128)(2,1)S(1)}, u32[]{:S(2)}, u32[]{:S(2)}) async-start(bf16[32,8,128]{2,1,0:T(8,128)(2,1)} %shard_map.135), calls=%async_computation | async-start | bytes 131072 | tf_op jit(solution)/shard_map/all_to_all | solution.py:266
  65.7 0.8 constant_dynamic-slice_fusion
  66.4 3.3 %collective-permute-start.2 = (bf16[128,4,128]{2,1,0:T(4,128)(2,1)S(1)}, bf16[128,4,128]{2,1,0:T(4,128)(2,1)S(1)}, u32[]{:S(2)}, u32[]{:S(2)}) collective-permute-start(bf16[128,4,128]{2,1,0:T(4,128)(2,1)S(1)} %get-tuple-element.19), channel_id=1, source_target_pairs={{0,8},{8,0},{1,9},{9,1},{2,10},{10,2},{3,11},{11,3},{4,12},{12,4},... | collective-permute-start | bytes 393224 | tf_op jit(solution)/shard_map/ppermute | solution.py:254
  69.7 10.4 %collective-permute-done.2.after_ref = bf16[128,4,128]{2,1,0:T(4,128)(2,1)S(1)} collective-permute-done((bf16[128,4,128]{2,1,0:T(4,128)(2,1)S(1)}, bf16[128,4,128]{2,1,0:T(4,128)(2,1)S(1)}, u32[]{:S(2)}, u32[]{:S(2)}) %collective-permute-start.2) | collective-permute-done | bytes 131104 | tf_op jit(solution)/shard_map/ppermute | solution.py:254
  80.1 0.7 all-to-all-done.in_ref
  80.8 0.7 shard_map.136
  81.5 9.6 %all-to-all-start.1 = ((f32[32,4,128]{2,1,0:T(4,128)}), f32[32,4,128]{2,1,0:T(4,128)S(1)}, u32[]{:S(2)}, u32[]{:S(2)}) async-start(f32[32,4,128]{2,1,0:T(4,128)} %shard_map.136), calls=%async_computation.1 | async-start | bytes 131072 | tf_op jit(solution)/shard_map/all_to_all | solution.py:270
  91.1 0.1 pad_add_fusion.place_ref.after_ref
  91.2 1.6 %copy-done.11 = bf16[32,2,128,128]{3,2,1,0:T(8,128)(2,1)S(1)} copy-done((bf16[32,2,128,128]{3,2,1,0:T(8,128)(2,1)S(1)}, bf16[32,2,128,128]{3,2,1,0:T(8,128)(2,1)}, u32[]{:S(2)}) %copy-start.11) | copy-done | bytes 2097176
  92.8 2.0 %shard_map.132 = bf16[512,128]{1,0:T(8,128)(2,1)} custom-call(s32[3]{0:T(128)S(1)} %pad_add_fusion.place_ref.after_ref, bf16[512,128]{1,0:T(8,128)(2,1)S(1)} %bitcast.51, bf16[8,2,2,2,128,128]{5,4,3,2,1,0:T(8,128)(2,1)S(1)} %bitcast.55, s32[3]{0:T(128)S(1)} %pad_add_fusion.place_ref.after_ref), custom_call_target="tpu_custom_call" | custom-call | flops 1073741824 | bytes 16777216 | tf_op jit(solution)/shard_map/pallas_call | solution.py:22
  94.8 4.2 %collective-permute-start.3 = (bf16[128,4,128]{2,1,0:T(4,128)(2,1)}, bf16[128,4,128]{2,1,0:T(4,128)(2,1)S(1)}, u32[]{:S(2)}, u32[]{:S(2)}) collective-permute-start(bf16[128,4,128]{2,1,0:T(4,128)(2,1)} %bitcast.18.after_ref), channel_id=1, source_target_pairs={{0,136},{8,128},{128,264},{136,256},{256,392},{264,384},{384,520},... | collective-permute-start | bytes 393224 | tf_op jit(solution)/shard_map/ppermute | solution.py:289
  99.1 5.1 %all-to-all-done.1.enter_ref = f32[32,4,128]{2,1,0:T(4,128)S(1)} async-done(((f32[32,4,128]{2,1,0:T(4,128)}), f32[32,4,128]{2,1,0:T(4,128)S(1)}, u32[]{:S(2)}, u32[]{:S(2)}) %all-to-all-start.1) | async-done | bytes 65568 | tf_op jit(solution)/shard_map/all_to_all | solution.py:270
  104.2 4.1 %shard_map.137 = bf16[128,2048]{1,0:T(8,128)(2,1)S(1)} custom-call(f32[128,2048]{1,0:T(8,128)S(1)} %shard_map.134.step_ref, bf16[128,2048]{1,0:T(8,128)(2,1)S(1)} %get-tuple-element.14.act_ref, f32[128,8,128]{2,1,0:T(8,128)S(1)} %broadcast_in_dim.13.entry_ref, f32[128,16]{1,0:T(8,128)S(1)} %psum.7.read_ref, f32[8,2048]{1,0:T(8,128)S(1)} %bitcast.48, ...), custom_call_target="tpu_custom_call" | custom-call | bytes 16777216 | tf_op jit(solution)/shard_map/pallas_call | solution.py:22
  108.3 3.2 %collective-permute-start.5 = (bf16[128,2048]{1,0:T(8,128)(2,1)S(1)}, bf16[128,2048]{1,0:T(8,128)(2,1)S(1)}, u32[]{:S(2)}, u32[]{:S(2)}) collective-permute-start(bf16[128,2048]{1,0:T(8,128)(2,1)S(1)} %shard_map.137), channel_id=1, source_target_pairs={{0,128},{128,256},{256,384},{384,512},{512,640},{640,768},{768,896... | collective-permute-start | bytes 1572872 | tf_op jit(solution)/shard_map/ppermute | solution.py:302
  111.5 0.0 collective-permute-done.3.after_ref
  111.5 0.0 copy-start.5
  111.6 0.9 copy-done.5
  112.4 1.3 shard_map.133
  113.8 3.4 %collective-permute-start.4 = (bf16[128,4,128]{2,1,0:T(4,128)(2,1)S(1)}, bf16[128,4,128]{2,1,0:T(4,128)(2,1)S(1)}, u32[]{:S(2)}, u32[]{:S(2)}) collective-permute-start(bf16[128,4,128]{2,1,0:T(4,128)(2,1)S(1)} %bitcast.57), channel_id=1, source_target_pairs={{0,128},{128,256},{256,384},{384,512},{512,640},{640,768},{768,896... | collective-permute-start | bytes 393224 | tf_op jit(solution)/shard_map/ppermute | solution.py:304
  117.2 9.8 %collective-permute-done.4 = bf16[128,4,128]{2,1,0:T(4,128)(2,1)S(1)} collective-permute-done((bf16[128,4,128]{2,1,0:T(4,128)(2,1)S(1)}, bf16[128,4,128]{2,1,0:T(4,128)(2,1)S(1)}, u32[]{:S(2)}, u32[]{:S(2)}) %collective-permute-start.4) | collective-permute-done | bytes 131104 | tf_op jit(solution)/shard_map/ppermute | solution.py:304
  127.1 0.8 maximum_bitcast_fusion
  127.9 0.0 collective-permute-done.5
  127.9 0.8 copy.33
  (18 shorter events, 0.1 us)
Async XLA Ops:
  7.2 84.0 %all-gather.3.cloned.1.call-start = ((), (), s32[]{:S(2)}) async-start(), calls=%async_computation.2 | async-start | bytes 2228224 | tf_op jit(solution)/shard_map/all_gather | solution.py:234
  8.1 16.2 %collective-permute-start.1 = (bf16[16,2048]{1,0:T(8,128)(2,1)S(1)}, bf16[16,2048]{1,0:T(8,128)(2,1)S(1)}, u32[]{:S(2)}, u32[]{:S(2)}) collective-permute-start(bf16[16,2048]{1,0:T(8,128)(2,1)S(1)} %slice_bitcast_fusion), channel_id=1, source_target_pairs={{0,4},{4,8},{8,12},{12,16},{16,20},{20,24},{24,28},{28,32},{32,36}... | collective-permute-start | bytes 196616 | tf_op jit(solution)/shard_map/ppermute | solution.py:232
  14.7 14.3 %copy-start.1 = (bf16[1,128,2048]{2,1,0:T(8,128)(2,1)S(1)}, bf16[1,128,2048]{2,1,0:T(8,128)(2,1)}, u32[]{:S(2)}) copy-start(bf16[1,128,2048]{2,1,0:T(8,128)(2,1)} %param.14) | copy-start | bytes 1572868
  14.7 14.3 %copy-start.6 = (bf16[1,2048,16]{1,2,0:T(8,128)(2,1)S(1)}, bf16[1,2048,16]{1,2,0:T(8,128)(2,1)}, u32[]{:S(2)}) copy-start(bf16[1,2048,16]{1,2,0:T(8,128)(2,1)} %param.22) | copy-start | bytes 196612
  14.7 14.3 %copy-start.7 = (f32[1,4,2048]{2,1,0:T(4,128)S(1)}, f32[1,4,2048]{2,1,0:T(4,128)}, u32[]{:S(2)}) copy-start(f32[1,4,2048]{2,1,0:T(4,128)} %param.20) | copy-start | bytes 98308
  14.7 14.3 %copy-start.9 = (f32[1,2048]{1,0:T(1,128)S(1)}, f32[1,2048]{1,0:T(1,128)}, u32[]{:S(2)}) copy-start(f32[1,2048]{1,0:T(1,128)} %bias_ref.2) | copy-start | bytes 24580
  14.8 9.4 %collective-permute-start = (bf16[2,128,128]{2,1,0:T(8,128)(2,1)S(1)}, bf16[2,128,128]{2,1,0:T(8,128)(2,1)S(1)}, u32[]{:S(2)}, u32[]{:S(2)}) collective-permute-start(bf16[2,128,128]{2,1,0:T(8,128)(2,1)S(1)} %bitcast.64), channel_id=1, source_target_pairs={{0,8},{8,0},{1,9},{9,1},{2,10},{10,2},{3,11},{11,3},{4,12},{12,4},... | collective-permute-start | bytes 196616 | tf_op jit(solution)/shard_map/ppermute | solution.py:231
  24.9 1.6 %copy-start = (bf16[1,512,2048]{2,1,0:T(8,128)(2,1)S(1)}, bf16[1,512,2048]{2,1,0:T(8,128)(2,1)}, u32[]{:S(2)}) copy-start(bf16[1,512,2048]{2,1,0:T(8,128)(2,1)} %param.17) | copy-start | bytes 6291460
  26.5 0.9 copy-start.4
  27.4 0.7 copy-start.8
  28.1 13.7 %copy-start.3 = (f32[1,8,2048]{2,1,0:T(8,128)S(1)}, f32[1,8,2048]{2,1,0:T(8,128)}, u32[]{:S(2)}) copy-start(f32[1,8,2048]{2,1,0:T(8,128)} %param.19) | copy-start | bytes 196612
  29.0 36.7 %copy-start.13 = (bf16[1,128,8,128]{3,2,1,0:T(8,128)(2,1)S(1)}, bf16[1,128,8,128]{3,2,1,0:T(8,128)(2,1)}, u32[]{:S(2)}) copy-start(bf16[1,128,8,128]{3,2,1,0:T(8,128)(2,1)} %param.12) | copy-start | bytes 786436
  45.5 35.3 %all-to-all-start = ((bf16[32,8,128]{2,1,0:T(8,128)(2,1)}), bf16[32,8,128]{2,1,0:T(8,128)(2,1)S(1)}, u32[]{:S(2)}, u32[]{:S(2)}) async-start(bf16[32,8,128]{2,1,0:T(8,128)(2,1)} %shard_map.135), calls=%async_computation | async-start | bytes 131072 | tf_op jit(solution)/shard_map/all_to_all | solution.py:266
  66.4 13.7 %collective-permute-start.2 = (bf16[128,4,128]{2,1,0:T(4,128)(2,1)S(1)}, bf16[128,4,128]{2,1,0:T(4,128)(2,1)S(1)}, u32[]{:S(2)}, u32[]{:S(2)}) collective-permute-start(bf16[128,4,128]{2,1,0:T(4,128)(2,1)S(1)} %get-tuple-element.19), channel_id=1, source_target_pairs={{0,8},{8,0},{1,9},{9,1},{2,10},{10,2},{3,11},{11,3},{4,12},{12,4},... | collective-permute-start | bytes 393224 | tf_op jit(solution)/shard_map/ppermute | solution.py:254
  81.5 22.7 %copy-start.2 = (bf16[1,128,2048]{2,1,0:T(8,128)(2,1)S(1)}, bf16[1,128,2048]{2,1,0:T(8,128)(2,1)}, u32[]{:S(2)}) copy-start(bf16[1,128,2048]{2,1,0:T(8,128)(2,1)} %param.15) | copy-start | bytes 1572868
  81.5 22.7 %copy-start.10 = (f32[1,2048]{1,0:T(1,128)S(1)}, f32[1,2048]{1,0:T(1,128)}, u32[]{:S(2)}) copy-start(f32[1,2048]{1,0:T(1,128)} %skip_ref.1) | copy-start | bytes 24580
  81.5 22.6 %all-to-all-start.1 = ((f32[32,4,128]{2,1,0:T(4,128)}), f32[32,4,128]{2,1,0:T(4,128)S(1)}, u32[]{:S(2)}, u32[]{:S(2)}) async-start(f32[32,4,128]{2,1,0:T(4,128)} %shard_map.136), calls=%async_computation.1 | async-start | bytes 131072 | tf_op jit(solution)/shard_map/all_to_all | solution.py:270
  91.2 1.6 %copy-start.11 = (bf16[32,2,128,128]{3,2,1,0:T(8,128)(2,1)S(1)}, bf16[32,2,128,128]{3,2,1,0:T(8,128)(2,1)}, u32[]{:S(2)}) copy-start(bf16[32,2,128,128]{3,2,1,0:T(8,128)(2,1)} %all-gather.3.cloned.1.call-done) | copy-start | bytes 6291460
  94.8 16.7 %collective-permute-start.3 = (bf16[128,4,128]{2,1,0:T(4,128)(2,1)}, bf16[128,4,128]{2,1,0:T(4,128)(2,1)S(1)}, u32[]{:S(2)}, u32[]{:S(2)}) collective-permute-start(bf16[128,4,128]{2,1,0:T(4,128)(2,1)} %bitcast.18.after_ref), channel_id=1, source_target_pairs={{0,136},{8,128},{128,264},{136,256},{256,392},{264,384},{384,520},... | collective-permute-start | bytes 393224 | tf_op jit(solution)/shard_map/ppermute | solution.py:289
  104.2 7.3 %copy-start.12 = (bf16[32,2,128,128]{3,2,1,0:T(8,128)(2,1)S(1)}, bf16[32,2,128,128]{3,2,1,0:T(8,128)(2,1)}, u32[]{:S(2)}) copy-start(bf16[32,2,128,128]{3,2,1,0:T(8,128)(2,1)} %all-gather.3.cloned.1.call-done) | copy-start | bytes 6291460
  108.3 19.6 %collective-permute-start.5 = (bf16[128,2048]{1,0:T(8,128)(2,1)S(1)}, bf16[128,2048]{1,0:T(8,128)(2,1)S(1)}, u32[]{:S(2)}, u32[]{:S(2)}) collective-permute-start(bf16[128,2048]{1,0:T(8,128)(2,1)S(1)} %shard_map.137), channel_id=1, source_target_pairs={{0,128},{128,256},{256,384},{384,512},{512,640},{640,768},{768,896... | collective-permute-start | bytes 1572872 | tf_op jit(solution)/shard_map/ppermute | solution.py:302
  111.5 0.9 copy-start.5
  113.8 13.2 %collective-permute-start.4 = (bf16[128,4,128]{2,1,0:T(4,128)(2,1)S(1)}, bf16[128,4,128]{2,1,0:T(4,128)(2,1)S(1)}, u32[]{:S(2)}, u32[]{:S(2)}) collective-permute-start(bf16[128,4,128]{2,1,0:T(4,128)(2,1)S(1)} %bitcast.57), channel_id=1, source_target_pairs={{0,128},{128,256},{256,384},{384,512},{512,640},{640,768},{768,896... | collective-permute-start | bytes 393224 | tf_op jit(solution)/shard_map/ppermute | solution.py:304
Sparse Core Ops, SparseCore 0:
  25.0 64.1 all-gather.2

commit v2 on v1

--- a/solution.py
+++ b/solution.py
@@ -30,7 +30,7 @@
     )(*args)
 
 
-def step_body(low_ref, weight_ref, bias_ref, step_ref):
+def step_body(low_ref, weight_ref, bias_ref, after_ref, step_ref):
     cols = weight_ref.shape[1]
     width = 512
     for at in range(0, cols, width):
@@ -43,7 +43,7 @@
     rows, cols = x_ref.shape
     taps = weight_ref.shape[0]
     width = 256
-    total = jnp.zeros(read_ref.shape, F32)
+    total = jnp.zeros(read_ref.shape[1:], F32)
     for at in range(0, cols, width):
         lanes = slice(at, at + width)
         padded = jnp.concatenate([halo_ref[:, lanes].astype(F32), x_ref[:, lanes].astype(F32)], axis=0)
@@ -54,19 +54,29 @@
         act = (v / (1.0 + jnp.exp(-v))).astype(BF16)
         act_ref[:, lanes] = act
         total = total + lax.dot_general(
-            act, proj_ref[:, lanes], (((1,), (1,)), ((), ())), preferred_element_type=F32
+            proj_ref[:, lanes], act, (((1,), (1,)), ((), ())), preferred_element_type=F32
         )
-    read_ref[...] = total
+    for part in range(read_ref.shape[0]):
+        read_ref[part] = total
 
 
 def wide(row, count):
     return jnp.broadcast_to(row, (count, row.shape[1]))
 
 
-def local_body(step_ref, act_ref, entry_ref, rate_ref, out_ref, drive_ref):
+def spread_entry(maps_ref, entry_ref):
+    maps = functools.reduce(jnp.add, [maps_ref[part] for part in range(maps_ref.shape[0])])
+    rows, count, lanes = entry_ref.shape
+    for row in range(rows):
+        entry_ref[row] = jnp.broadcast_to(maps[:count, row : row + 1], (count, lanes))
+    return maps
+
+
+def local_body(step_ref, act_ref, maps_ref, rate_ref, out_ref, drive_ref, entry_ref):
     rows, cols = step_ref.shape
     count = rate_ref.shape[0]
     drive_ref[...] = step_ref[...] * act_ref[...].astype(F32)
+    spread_entry(maps_ref, entry_ref)
     rate = rate_ref[...] * -LOG2E
 
     def block(at, carry):
@@ -101,16 +111,22 @@
         state = pair[half:] * state + pair[:half]
 
 
-def scan_body(step_ref, act_ref, entry_ref, read_ref, rate_ref, enter_ref, skip_ref, gate_ref, after_ref, out_ref, drive_ref, held_ref):
+def scan_body(
+    step_ref, act_ref, maps_ref, rate_ref, enter_ref, skip_ref, gate_ref, out_ref,
+    drive_ref, entry_ref, read_ref, held_ref,
+):
     rows, cols = step_ref.shape
     count = rate_ref.shape[0]
     span = held_ref.shape[0] // count
     drive_ref[...] = step_ref[...] * act_ref[...].astype(F32)
     rate = rate_ref[...] * -LOG2E
-    wanted = lax.broadcasted_iota(jnp.int32, (2 * count, span * count), 1) % count + count
-    spread = (lax.broadcasted_iota(jnp.int32, wanted.shape, 0) == wanted).astype(BF16)
-    held_at = lax.broadcasted_iota(jnp.int32, (span, span * count), 1) // count
-    own = held_at == lax.broadcasted_iota(jnp.int32, held_at.shape, 0)
+    maps = spread_entry(maps_ref, entry_ref)
+    shape = (count, span * count)
+    spread = (lax.broadcasted_iota(jnp.int32, shape, 0) == lax.broadcasted_iota(jnp.int32, shape, 1) % count)
+    read = jnp.dot(maps[count:].T.astype(BF16), spread.astype(BF16), preferred_element_type=F32)
+    held_at = lax.broadcasted_iota(jnp.int32, read.shape, 1) // count
+    own = held_at == lax.broadcasted_iota(jnp.int32, read.shape, 0) % span
+    read_ref[...] = jnp.where(own, read, 0.0).astype(BF16)
     state = jnp.concatenate(
         [
             jnp.concatenate([enter_ref[2 * block], enter_ref[2 * block + 1]], axis=0)
@@ -130,8 +146,7 @@
                 state = jnp.exp2(rate * step) * state + entry * drive
                 pair.append(state)
             held_ref[i * count : (i + 2) * count, :] = jnp.concatenate(pair, axis=0).astype(BF16)
-        read = jnp.dot(read_ref[pl.ds(base, span), :].astype(BF16), spread, preferred_element_type=F32)
-        read = jnp.where(own, read, 0.0).astype(BF16)
+        read = read_ref[pl.ds(base, span), :]
         width = 512
         for lane in range(0, cols, width):
             lanes = slice(lane, lane + width)
@@ -221,7 +236,7 @@
     group = heads // kv_heads
     cols = mamba_in.shape[1]
     count = decay_rate.shape[0]
-    taps = conv_weight.shape[1]
+    parts_tp = lax.axis_size("tp")
     pipes = lax.axis_size("pipe")
     places = lax.axis_size(CTX)
     zh, zc, core = (lax.axis_index(a) for a in CTX)
@@ -234,33 +249,32 @@
     kv = lax.all_gather(jnp.stack([own_kv, other_kv]), ("zh", "core"))
     kv = kv.reshape((lax.axis_size("zh"), lax.axis_size("core")) + kv.shape[1:])
 
-    step = kernel_call(
-        step_body,
-        jax.ShapeDtypeStruct((rows, cols), F32),
-        (step_low[0], step_weight[0], step_bias),
-        flops=2 * rows * cols * step_low.shape[2],
-        nbytes=4 << 20,
-    )
     act, partial = kernel_call(
         conv_body,
-        (jax.ShapeDtypeStruct((rows, cols), BF16), jax.ShapeDtypeStruct((rows, 2 * count), F32)),
+        (jax.ShapeDtypeStruct((rows, cols), BF16), jax.ShapeDtypeStruct((parts_tp, 2 * count, rows), F32)),
         (mamba_in, halo, conv_weight[0], conv_bias, state_weight.T),
         nbytes=4 << 20,
     )
-    entry_read = lax.psum(partial, "tp")
-    queries, entry_read = lax.optimization_barrier((queries, entry_read))
+    queries, _ = lax.optimization_barrier((queries, act))
     grouped = queries.reshape(rows, kv_heads, group, width)
     own_q = lax.dynamic_index_in_dim(grouped, zc, 1, False)
     other_q = lax.ppermute(lax.dynamic_index_in_dim(grouped, 1 - zc, 1, False), "zc", swap)
     place = jnp.stack([zh, zc, core]).astype(jnp.int32)
 
-    entry = jnp.broadcast_to(entry_read[:, :count, None], (rows, count, 128))
+    step = kernel_call(
+        step_body,
+        jax.ShapeDtypeStruct((rows, cols), F32),
+        (step_low[0], step_weight[0], step_bias, act),
+        flops=2 * rows * cols * step_low.shape[2],
+        nbytes=4 << 20,
+    )
+    maps = lax.all_to_all(partial, "tp", 0, 0, tiled=True)
     span = 32
     parts = kernel_call(
         local_body,
         jax.ShapeDtypeStruct((2 * cols // 128, count, 128), BF16),
-        (step, act, entry, decay_rate),
-        scratch=[pltpu.VMEM((rows, cols), F32)],
+        (step, act, maps, decay_rate),
+        scratch=[pltpu.VMEM((rows, cols), F32), pltpu.VMEM((rows, count, 128), F32)],
         nbytes=16 << 20,
     )
     parts = lax.all_to_all(parts, CTX, 0, 0, tiled=True)
@@ -275,7 +289,7 @@
             functools.partial(attend_body, slot=slot, group=group),
             jax.ShapeDtypeStruct((lines, width), BF16),
             (place, q.reshape(lines, width), kv, after),
-            specs=[SMEM, VMEM, VMEM, SMEM if after is place else VMEM],
+            specs=[SMEM, VMEM, VMEM, VMEM],
             scratch=[
                 pltpu.VMEM((places // 4, lines, keys), F32),
                 pltpu.VMEM((lines, width), F32),
@@ -285,22 +299,27 @@
             nbytes=16 << 20,
         ).reshape(rows, group, width)
 
-    far = attend(other_q, 1, place)
+    gated = kernel_call(
+        scan_body,
+        jax.ShapeDtypeStruct((rows, cols), BF16),
+        (step, act, maps, decay_rate, entering, skip_gain, gate_in),
+
+        scratch=[
+            pltpu.VMEM((rows, cols), F32),
+            pltpu.VMEM((rows, count, 128), F32),
+            pltpu.VMEM((rows, span * count), BF16),
+            pltpu.VMEM((span * count, cols), BF16),
+        ],
+        nbytes=16 << 20,
+    )
+    mamba_out = lax.ppermute(gated, "pipe", [(i, (i + 1) % pipes) for i in range(pipes)])
+    far = attend(other_q, 1, gated)
     far_sent = lax.ppermute(
         far,
         ("pipe", "zc"),
         [(2 * i + j, 2 * ((i + 1) % pipes) + 1 - j) for i in range(pipes) for j in range(2)],
     )
-    gated = kernel_call(
-        scan_body,
-        jax.ShapeDtypeStruct((rows, cols), BF16),
-        (step, act, entry, entry_read, decay_rate, entering, skip_gain, gate_in, far),
-
-        scratch=[pltpu.VMEM((rows, cols), F32), pltpu.VMEM((span * count, cols), BF16)],
-        nbytes=16 << 20,
-    )
-    mamba_out = lax.ppermute(gated, "pipe", [(i, (i + 1) % pipes) for i in range(pipes)])
-    near = attend(own_q, 0, far_sent)
+    near = attend(own_q, 0, gated)
     near = lax.ppermute(near, "pipe", [(i, (i + 1) % pipes) for i in range(pipes)])
     far = far_sent
     first = jnp.where(zc == 0, near, far)

time: 137 us -> 133 us (0.971)
  blocking collectives: 11.4 us -> 25.4 us
  waiting for transfers between devices: 31.4 us -> 22.1 us
  starting transfers between devices: 53.3 us -> 46.5 us
    all_to_all x0 -> x1, blocking collectives: none -> 25.4 us  [per_device(): entering = lax.all_to_all(entering, CTX, 0, 0, tiled=True)]
    psum x1 -> x0, blocking collectives: 11.4 us -> none  [per_device(): entry_read = lax.psum(partial, 'tp')]
    ppermute x1, starting transfers between devices: 5.38 us -> 14.8 us  [per_device(): lax.ppermute(mamba_in[rows - HALO:], CTX, [(i, i + 1) for i in range(plac...]
    all_to_all x1, starting transfers between devices: 20.1 us -> 11.8 us  [per_device(): parts = lax.all_to_all(parts, CTX, 0, 0, tiled=True)]
    ppermute x1, waiting for transfers between devices: 9.84 us -> 2.81 us  [per_device(): lax.ppermute(near, 'pipe', [(i, (i + 1) % pipes) for i in range(pipes)])]
    all_to_all x1, starting transfers between devices: 9.56 us -> 3.4 us  [per_device(): maps = lax.all_to_all(partial, 'tp', 0, 0, tiled=True)]
    ppermute x1, waiting for transfers between devices: 0.01 us -> 5.04 us  [per_device(): lax.ppermute(gated, 'pipe', [(i, (i + 1) % pipes) for i in range(pipes)])]
    ppermute x1, waiting for transfers between devices: 5.28 us -> 1.28 us  [per_device(): lax.ppermute(mamba_in[rows - HALO:], CTX, [(i, i + 1) for i in range(plac...]
  transfers between devices with their start and end apart: 9 -> 9, of which waited for: 5 -> 6; matrix products, arithmetic and copies ran while one was open for 2% -> 1% of each run, Pallas kernels for 10% -> 10%
where the time goes in v2:
time: 133 us; the launch traced here: 132 us
  starting transfers between devices  46.5 us (35%)
  blocking collectives  25.4 us (19%)
  waiting for transfers between devices  22.1 us (17%)
  between operations  14.3 us (11%)
  Pallas kernels  12.9 us (10%)
  local copies, waits for them, and re-layouts  9.56 us (7%)
  other arithmetic  1.61 us (1%)
    all_to_all x1, blocking collectives, per_device(): entering = lax.all_to_all(entering, CTX, 0, 0, tiled=True)  25.4 us
    ppermute x1, starting transfers between devices, per_device(): lax.ppermute(mamba_in[rows - HALO:], CTX, [(i, i + 1) for i in range(plac...  14.8 us
    pallas_call x7, Pallas kernels, kernel_call(): pl.pallas_call(body, out_shape=out_shape, in_specs=specs or [VMEM] * len(...  12.9 us
    all_to_all x1, starting transfers between devices, per_device(): parts = lax.all_to_all(parts, CTX, 0, 0, tiled=True)  11.8 us
    ppermute x1, waiting for transfers between devices, per_device(): lax.ppermute(lax.dynamic_index_in_dim(grouped, 1 - zc, 1, False), 'zc', s...  11 us
    unnamed x27, local copies, waits for them, and re-layouts  7.35 us
    ppermute x1, waiting for transfers between devices, per_device(): lax.ppermute(gated, 'pipe', [(i, (i + 1) % pipes) for i in range(pipes)])  5.04 us
    ppermute x1, starting transfers between devices, per_device(): lax.ppermute(lax.dynamic_index_in_dim(key_value, 1 - zc, 2, False), 'zc',...  4.83 us
  transfers between devices with their start and end apart: 9, of which 6 were waited for; matrix products, arithmetic and copies ran while one was open for 1% of the time, Pallas kernels for 10%

profile of v2, /device:TPU:1, one launch (start us, length us, event | category | flops | bytes accessed | tf_op | source)
XLA Modules:
  0.0 132.2 jit_solution(18397496063903679335)
XLA Ops:
  7.2 0.0 copy-start.4
  7.2 0.0 copy-start.8
  7.2 0.0 all-gather.3.cloned.1.call-start
  7.2 1.3 constant_dynamic-slice_fusion.1
  8.5 4.8 %collective-permute-start = (bf16[2,128,128]{2,1,0:T(8,128)(2,1)S(1)}, bf16[2,128,128]{2,1,0:T(8,128)(2,1)S(1)}, u32[]{:S(2)}, u32[]{:S(2)}) collective-permute-start(bf16[2,128,128]{2,1,0:T(8,128)(2,1)S(1)} %bitcast.63), channel_id=1, source_target_pairs={{0,8},{8,0},{1,9},{9,1},{2,10},{10,2},{3,11},{11,3},{4,12},{12,4},... | collective-permute-start | bytes 196616 | tf_op jit(solution)/shard_map/ppermute | solution.py:246
  13.4 0.8 slice_bitcast_fusion
  14.2 14.8 %collective-permute-start.1 = (bf16[16,2048]{1,0:T(8,128)(2,1)S(1)}, bf16[16,2048]{1,0:T(8,128)(2,1)S(1)}, u32[]{:S(2)}, u32[]{:S(2)}) collective-permute-start(bf16[16,2048]{1,0:T(8,128)(2,1)S(1)} %slice_bitcast_fusion), channel_id=1, source_target_pairs={{0,4},{4,8},{8,12},{12,16},{16,20},{20,24},{24,28},{28,32},{32,36}... | collective-permute-start | bytes 196616 | tf_op jit(solution)/shard_map/ppermute | solution.py:247
  29.0 0.0 collective-permute-done
  29.0 1.3 collective-permute-done.1.halo_ref
  30.3 0.7 pad_maximum_fusion
  31.0 0.0 all-gather.3.cloned.1.call-update
  31.0 0.0 copy-start.1
  31.0 1.0 copy-done.1
  32.0 0.8 copy-done.5
  32.9 0.8 copy-done.6
  33.6 0.7 copy-done.7
  34.3 1.8 %shard_map.131 = (bf16[128,2048]{1,0:T(8,128)(2,1)S(1)}, f32[4,16,128]{2,1,0:T(8,128)}) custom-call(bf16[128,2048]{1,0:T(8,128)(2,1)S(1)} %bitcast.43, bf16[16,2048]{1,0:T(8,128)(2,1)S(1)} %collective-permute-done.1.halo_ref, f32[4,2048]{1,0:T(4,128)S(1)} %bitcast.51, f32[1,2048]{1,0:T(1,128)S(1)} %copy-done.7, bf16[16,2048]{1,0:T(8,128)(2,1)S(1)} %bitcast.50), custom_call_target="tpu_custom_call" | custom-call | bytes 4194304 | tf_op jit(solution)/shard_map/pallas_call | solution.py:22
  36.1 3.4 %all-to-all-start = ((f32[4,16,128]{2,1,0:T(8,128)}), f32[4,16,128]{2,1,0:T(8,128)S(1)}, u32[]{:S(2)}, u32[]{:S(2)}) async-start(f32[4,16,128]{2,1,0:T(8,128)} %get-tuple-element.13), calls=%async_computation | async-start | bytes 65536 | tf_op jit(solution)/shard_map/all_to_all | solution.py:271
  39.5 0.0 copy-done.4
  39.6 0.0 copy-done.8
  39.6 0.0 copy-start
  39.6 1.6 %copy-done = bf16[1,512,2048]{2,1,0:T(8,128)(2,1)S(1)} copy-done((bf16[1,512,2048]{2,1,0:T(8,128)(2,1)S(1)}, bf16[1,512,2048]{2,1,0:T(8,128)(2,1)}, u32[]{:S(2)}) %copy-start) | copy-done | bytes 2097176
  41.2 0.9 shard_map.132.step_ref
  42.0 0.0 copy-start.2
  42.0 0.0 copy-start.9
  42.0 1.8 %all-to-all-done.maps_ref = f32[4,16,128]{2,1,0:T(8,128)S(1)} async-done(((f32[4,16,128]{2,1,0:T(8,128)}), f32[4,16,128]{2,1,0:T(8,128)S(1)}, u32[]{:S(2)}, u32[]{:S(2)}) %all-to-all-start) | async-done | bytes 32800 | tf_op jit(solution)/shard_map/all_to_all | solution.py:271
  43.8 4.0 %shard_map.133 = bf16[32,8,128]{2,1,0:T(8,128)(2,1)} custom-call(f32[128,2048]{1,0:T(8,128)S(1)} %shard_map.132.step_ref, bf16[128,2048]{1,0:T(8,128)(2,1)S(1)} %get-tuple-element.9.after_ref.act_ref, f32[4,16,128]{2,1,0:T(8,128)S(1)} %all-to-all-done.maps_ref, f32[8,2048]{1,0:T(8,128)S(1)} %bitcast.45), custom_call_target="tpu_custom_call" | custom-call | bytes 16777216 | tf_op jit(solution)/shard_map/pallas_call | solution.py:22
  47.8 11.8 %all-to-all-start.1 = ((bf16[32,8,128]{2,1,0:T(8,128)(2,1)}), bf16[32,8,128]{2,1,0:T(8,128)(2,1)S(1)}, u32[]{:S(2)}, u32[]{:S(2)}) async-start(bf16[32,8,128]{2,1,0:T(8,128)(2,1)} %shard_map.133), calls=%async_computation.1 | async-start | bytes 131072 | tf_op jit(solution)/shard_map/all_to_all | solution.py:280
  59.7 0.1 constant_dynamic-slice_fusion
  59.8 3.3 %collective-permute-start.2 = (bf16[128,4,128]{2,1,0:T(4,128)(2,1)S(1)}, bf16[128,4,128]{2,1,0:T(4,128)(2,1)S(1)}, u32[]{:S(2)}, u32[]{:S(2)}) collective-permute-start(bf16[128,4,128]{2,1,0:T(4,128)(2,1)S(1)} %get-tuple-element.17), channel_id=1, source_target_pairs={{0,8},{8,0},{1,9},{9,1},{2,10},{10,2},{3,11},{11,3},{4,12},{12,4},... | collective-permute-start | bytes 393224 | tf_op jit(solution)/shard_map/ppermute | solution.py:261
  63.1 11.0 %collective-permute-done.2.after_ref = bf16[128,4,128]{2,1,0:T(4,128)(2,1)S(1)} collective-permute-done((bf16[128,4,128]{2,1,0:T(4,128)(2,1)S(1)}, bf16[128,4,128]{2,1,0:T(4,128)(2,1)S(1)}, u32[]{:S(2)}, u32[]{:S(2)}) %collective-permute-start.2) | collective-permute-done | bytes 131104 | tf_op jit(solution)/shard_map/ppermute | solution.py:261
  74.1 0.2 all-to-all-done.1.in_ref
  74.3 0.1 shard_map.134
  74.3 25.4 %all_to_all.15.enter_ref = f32[32,4,128]{2,1,0:T(4,128)S(1)} all-to-all(f32[32,4,128]{2,1,0:T(4,128)S(1)} %shard_map.134), channel_id=1, replica_groups=mesh['pipe'=8,'zh'=8,'zc'=2,'core'=2,'tp'=4] {'zh','zc','core'}, dimensions={0} | all-to-all | bytes 131072 | tf_op jit(solution)/shard_map/all_to_all | solution.py:284
  99.8 0.0 copy-done.2
  99.8 3.4 %shard_map.135.after_ref = bf16[128,2048]{1,0:T(8,128)(2,1)S(1)} custom-call(f32[128,2048]{1,0:T(8,128)S(1)} %shard_map.132.step_ref, bf16[128,2048]{1,0:T(8,128)(2,1)S(1)} %get-tuple-element.9.after_ref.act_ref, f32[4,16,128]{2,1,0:T(8,128)S(1)} %all-to-all-done.maps_ref, f32[8,2048]{1,0:T(8,128)S(1)} %bitcast.46, f32[32,4,128]{2,1,0:T(4,128)S(1)} %all_to_all.15.enter_ref, ...), custom_call_target="tpu_custom_call" | custom-call | bytes 16777216 | tf_op jit(solution)/shard_map/pallas_call | solution.py:22
  103.2 2.0 %collective-permute-start.5 = (bf16[128,2048]{1,0:T(8,128)(2,1)S(1)}, bf16[128,2048]{1,0:T(8,128)(2,1)S(1)}, u32[]{:S(2)}, u32[]{:S(2)}) collective-permute-start(bf16[128,2048]{1,0:T(8,128)(2,1)S(1)} %shard_map.135.after_ref), channel_id=1, source_target_pairs={{0,128},{128,256},{256,384},{384,512},{512,640},{640,768},{768,896... | collective-permute-start | bytes 1572872 | tf_op jit(solution)/shard_map/ppermute | solution.py:315
  105.2 0.1 pad_add_fusion.place_ref
  105.3 1.6 %copy-done.10 = bf16[32,2,128,128]{3,2,1,0:T(8,128)(2,1)S(1)} copy-done((bf16[32,2,128,128]{3,2,1,0:T(8,128)(2,1)S(1)}, bf16[32,2,128,128]{3,2,1,0:T(8,128)(2,1)}, u32[]{:S(2)}) %copy-start.10) | copy-done | bytes 2097176
  106.9 1.4 %shard_map.137 = bf16[512,128]{1,0:T(8,128)(2,1)S(1)} custom-call(s32[3]{0:T(128)S(1)} %pad_add_fusion.place_ref, bf16[512,128]{1,0:T(8,128)(2,1)S(1)} %bitcast.47, bf16[8,2,2,2,128,128]{5,4,3,2,1,0:T(8,128)(2,1)S(1)} %bitcast.52, bf16[128,2048]{1,0:T(8,128)(2,1)S(1)} %shard_map.135.after_ref), custom_call_target="tpu_custom_call" | custom-call | flops 1073741824 | bytes 16777216 | tf_op jit(solution)/shard_map/pallas_call | solution.py:22
  108.2 3.4 %collective-permute-start.4 = (bf16[128,4,128]{2,1,0:T(4,128)(2,1)S(1)}, bf16[128,4,128]{2,1,0:T(4,128)(2,1)S(1)}, u32[]{:S(2)}, u32[]{:S(2)}) collective-permute-start(bf16[128,4,128]{2,1,0:T(4,128)(2,1)S(1)} %bitcast.54), channel_id=1, source_target_pairs={{0,136},{8,128},{128,264},{136,256},{256,392},{264,384},{384,520},... | collective-permute-start | bytes 393224 | tf_op jit(solution)/shard_map/ppermute | solution.py:317
  111.6 1.3 %shard_map.136 = bf16[512,128]{1,0:T(8,128)(2,1)S(1)} custom-call(s32[3]{0:T(128)S(1)} %pad_add_fusion.place_ref, bf16[512,128]{1,0:T(8,128)(2,1)S(1)} %bitcast.48, bf16[8,2,2,2,128,128]{5,4,3,2,1,0:T(8,128)(2,1)S(1)} %bitcast.53, bf16[128,2048]{1,0:T(8,128)(2,1)S(1)} %shard_map.135.after_ref), custom_call_target="tpu_custom_call" | custom-call | flops 1073741824 | bytes 16777216 | tf_op jit(solution)/shard_map/pallas_call | solution.py:22
  113.0 2.9 %collective-permute-start.3 = (bf16[128,4,128]{2,1,0:T(4,128)(2,1)S(1)}, bf16[128,4,128]{2,1,0:T(4,128)(2,1)S(1)}, u32[]{:S(2)}, u32[]{:S(2)}) collective-permute-start(bf16[128,4,128]{2,1,0:T(4,128)(2,1)S(1)} %bitcast.55), channel_id=1, source_target_pairs={{0,128},{128,256},{256,384},{384,512},{512,640},{640,768},{768,896... | collective-permute-start | bytes 393224 | tf_op jit(solution)/shard_map/ppermute | solution.py:323
  115.9 5.0 %collective-permute-done.5 = bf16[128,2048]{1,0:T(8,128)(2,1)S(1)} collective-permute-done((bf16[128,2048]{1,0:T(8,128)(2,1)S(1)}, bf16[128,2048]{1,0:T(8,128)(2,1)S(1)}, u32[]{:S(2)}, u32[]{:S(2)}) %collective-permute-start.5) | collective-permute-done | bytes 524320 | tf_op jit(solution)/shard_map/ppermute | solution.py:315
  120.9 0.0 collective-permute-done.4
  120.9 2.8 %collective-permute-done.3 = bf16[128,4,128]{2,1,0:T(4,128)(2,1)S(1)} collective-permute-done((bf16[128,4,128]{2,1,0:T(4,128)(2,1)S(1)}, bf16[128,4,128]{2,1,0:T(4,128)(2,1)S(1)}, u32[]{:S(2)}, u32[]{:S(2)}) %collective-permute-start.3) | collective-permute-done | bytes 131104 | tf_op jit(solution)/shard_map/ppermute | solution.py:323
  123.8 0.8 maximum_bitcast_fusion
  124.6 0.8 copy.33
  (13 shorter events, 0.1 us)
Async XLA Ops:
  7.2 32.4 %copy-start.4 = (bf16[1,128,512]{2,1,0:T(8,128)(2,1)S(1)}, bf16[1,128,512]{2,1,0:T(8,128)(2,1)}, u32[]{:S(2)}) copy-start(bf16[1,128,512]{2,1,0:T(8,128)(2,1)} %param.16) | copy-start | bytes 393220
  7.2 32.4 %copy-start.8 = (f32[1,2048]{1,0:T(1,128)S(1)}, f32[1,2048]{1,0:T(1,128)}, u32[]{:S(2)}) copy-start(f32[1,2048]{1,0:T(1,128)} %bias_ref.3) | copy-start | bytes 24580
  7.2 98.1 %all-gather.3.cloned.1.call-start = ((), (), s32[]{:S(2)}) async-start(), calls=%async_computation.3 | async-start | bytes 2228224 | tf_op jit(solution)/shard_map/all_gather | solution.py:249
  8.5 20.5 %collective-permute-start = (bf16[2,128,128]{2,1,0:T(8,128)(2,1)S(1)}, bf16[2,128,128]{2,1,0:T(8,128)(2,1)S(1)}, u32[]{:S(2)}, u32[]{:S(2)}) collective-permute-start(bf16[2,128,128]{2,1,0:T(8,128)(2,1)S(1)} %bitcast.63), channel_id=1, source_target_pairs={{0,8},{8,0},{1,9},{9,1},{2,10},{10,2},{3,11},{11,3},{4,12},{12,4},... | collective-permute-start | bytes 196616 | tf_op jit(solution)/shard_map/ppermute | solution.py:246
  14.2 16.1 %collective-permute-start.1 = (bf16[16,2048]{1,0:T(8,128)(2,1)S(1)}, bf16[16,2048]{1,0:T(8,128)(2,1)S(1)}, u32[]{:S(2)}, u32[]{:S(2)}) collective-permute-start(bf16[16,2048]{1,0:T(8,128)(2,1)S(1)} %slice_bitcast_fusion), channel_id=1, source_target_pairs={{0,4},{4,8},{8,12},{12,16},{16,20},{20,24},{24,28},{28,32},{32,36}... | collective-permute-start | bytes 196616 | tf_op jit(solution)/shard_map/ppermute | solution.py:247
  31.0 1.0 copy-start.1
  32.0 0.8 copy-start.5
  32.9 0.8 copy-start.6
  33.6 0.7 copy-start.7
  36.1 7.7 %copy-start.3 = (f32[1,8,2048]{2,1,0:T(8,128)S(1)}, f32[1,8,2048]{2,1,0:T(8,128)}, u32[]{:S(2)}) copy-start(f32[1,8,2048]{2,1,0:T(8,128)} %param.19) | copy-start | bytes 196612
  36.1 7.7 %all-to-all-start = ((f32[4,16,128]{2,1,0:T(8,128)}), f32[4,16,128]{2,1,0:T(8,128)S(1)}, u32[]{:S(2)}, u32[]{:S(2)}) async-start(f32[4,16,128]{2,1,0:T(8,128)} %get-tuple-element.13), calls=%async_computation | async-start | bytes 65536 | tf_op jit(solution)/shard_map/all_to_all | solution.py:271
  39.6 1.6 %copy-start = (bf16[1,512,2048]{2,1,0:T(8,128)(2,1)S(1)}, bf16[1,512,2048]{2,1,0:T(8,128)(2,1)}, u32[]{:S(2)}) copy-start(bf16[1,512,2048]{2,1,0:T(8,128)(2,1)} %param.17) | copy-start | bytes 6291460
  41.2 18.5 %copy-start.11 = (bf16[1,128,8,128]{3,2,1,0:T(8,128)(2,1)S(1)}, bf16[1,128,8,128]{3,2,1,0:T(8,128)(2,1)}, u32[]{:S(2)}) copy-start(bf16[1,128,8,128]{3,2,1,0:T(8,128)(2,1)} %param.12) | copy-start | bytes 786436
  42.0 57.7 %copy-start.2 = (bf16[1,128,2048]{2,1,0:T(8,128)(2,1)S(1)}, bf16[1,128,2048]{2,1,0:T(8,128)(2,1)}, u32[]{:S(2)}) copy-start(bf16[1,128,2048]{2,1,0:T(8,128)(2,1)} %param.15) | copy-start | bytes 1572868
  42.0 57.7 %copy-start.9 = (f32[1,2048]{1,0:T(1,128)S(1)}, f32[1,2048]{1,0:T(1,128)}, u32[]{:S(2)}) copy-start(f32[1,2048]{1,0:T(1,128)} %skip_ref.1) | copy-start | bytes 24580
  47.8 26.4 %all-to-all-start.1 = ((bf16[32,8,128]{2,1,0:T(8,128)(2,1)}), bf16[32,8,128]{2,1,0:T(8,128)(2,1)S(1)}, u32[]{:S(2)}, u32[]{:S(2)}) async-start(bf16[32,8,128]{2,1,0:T(8,128)(2,1)} %shard_map.133), calls=%async_computation.1 | async-start | bytes 131072 | tf_op jit(solution)/shard_map/all_to_all | solution.py:280
  59.8 14.3 %collective-permute-start.2 = (bf16[128,4,128]{2,1,0:T(4,128)(2,1)S(1)}, bf16[128,4,128]{2,1,0:T(4,128)(2,1)S(1)}, u32[]{:S(2)}, u32[]{:S(2)}) collective-permute-start(bf16[128,4,128]{2,1,0:T(4,128)(2,1)S(1)} %get-tuple-element.17), channel_id=1, source_target_pairs={{0,8},{8,0},{1,9},{9,1},{2,10},{10,2},{3,11},{11,3},{4,12},{12,4},... | collective-permute-start | bytes 393224 | tf_op jit(solution)/shard_map/ppermute | solution.py:261
  103.2 17.8 %collective-permute-start.5 = (bf16[128,2048]{1,0:T(8,128)(2,1)S(1)}, bf16[128,2048]{1,0:T(8,128)(2,1)S(1)}, u32[]{:S(2)}, u32[]{:S(2)}) collective-permute-start(bf16[128,2048]{1,0:T(8,128)(2,1)S(1)} %shard_map.135.after_ref), channel_id=1, source_target_pairs={{0,128},{128,256},{256,384},{384,512},{512,640},{640,768},{768,896... | collective-permute-start | bytes 1572872 | tf_op jit(solution)/shard_map/ppermute | solution.py:315
  105.3 1.6 %copy-start.10 = (bf16[32,2,128,128]{3,2,1,0:T(8,128)(2,1)S(1)}, bf16[32,2,128,128]{3,2,1,0:T(8,128)(2,1)}, u32[]{:S(2)}) copy-start(bf16[32,2,128,128]{3,2,1,0:T(8,128)(2,1)} %all-gather.3.cloned.1.call-done) | copy-start | bytes 6291460
  108.2 12.7 %collective-permute-start.4 = (bf16[128,4,128]{2,1,0:T(4,128)(2,1)S(1)}, bf16[128,4,128]{2,1,0:T(4,128)(2,1)S(1)}, u32[]{:S(2)}, u32[]{:S(2)}) collective-permute-start(bf16[128,4,128]{2,1,0:T(4,128)(2,1)S(1)} %bitcast.54), channel_id=1, source_target_pairs={{0,136},{8,128},{128,264},{136,256},{256,392},{264,384},{384,520},... | collective-permute-start | bytes 393224 | tf_op jit(solution)/shard_map/ppermute | solution.py:317
  113.0 10.8 %collective-permute-start.3 = (bf16[128,4,128]{2,1,0:T(4,128)(2,1)S(1)}, bf16[128,4,128]{2,1,0:T(4,128)(2,1)S(1)}, u32[]{:S(2)}, u32[]{:S(2)}) collective-permute-start(bf16[128,4,128]{2,1,0:T(4,128)(2,1)S(1)} %bitcast.55), channel_id=1, source_target_pairs={{0,128},{128,256},{256,384},{384,512},{512,640},{640,768},{768,896... | collective-permute-start | bytes 393224 | tf_op jit(solution)/shard_map/ppermute | solution.py:323
Sparse Core Ops, SparseCore 0:
  31.1 57.7 all-gather.2

commit v3 on v2

--- a/solution.py
+++ b/solution.py
@@ -101,7 +101,7 @@
         out_ref[part] = both.astype(out_ref.dtype)
 
 
-def prefix_body(in_ref, after_ref, out_ref):
+def prefix_body(in_ref, out_ref):
     places, both, lanes = in_ref.shape
     half = both // 2
     state = jnp.zeros((half, lanes), F32)
@@ -111,22 +111,27 @@
         state = pair[half:] * state + pair[:half]
 
 
+def read_body(maps_ref, asked_ref, after_ref, out_ref):
+    count = maps_ref.shape[1] // 2
+    shape = (count, out_ref.shape[1])
+    maps = functools.reduce(jnp.add, [maps_ref[part, count:] for part in range(maps_ref.shape[0])])
+    spread = lax.broadcasted_iota(jnp.int32, shape, 0) == lax.broadcasted_iota(jnp.int32, shape, 1) % count
+    read = jnp.dot(maps.T.astype(BF16), spread.astype(BF16), preferred_element_type=F32)
+    held_at = lax.broadcasted_iota(jnp.int32, read.shape, 1) // count
+    own = held_at == lax.broadcasted_iota(jnp.int32, read.shape, 0) % (shape[1] // count)
+    out_ref[...] = jnp.where(own, read, 0.0).astype(BF16)
+
+
 def scan_body(
-    step_ref, act_ref, maps_ref, rate_ref, enter_ref, skip_ref, gate_ref, out_ref,
-    drive_ref, entry_ref, read_ref, held_ref,
+    step_ref, act_ref, maps_ref, read_ref, rate_ref, enter_ref, skip_ref, gate_ref, out_ref,
+    drive_ref, entry_ref, held_ref,
 ):
     rows, cols = step_ref.shape
     count = rate_ref.shape[0]
     span = held_ref.shape[0] // count
     drive_ref[...] = step_ref[...] * act_ref[...].astype(F32)
     rate = rate_ref[...] * -LOG2E
-    maps = spread_entry(maps_ref, entry_ref)
-    shape = (count, span * count)
-    spread = (lax.broadcasted_iota(jnp.int32, shape, 0) == lax.broadcasted_iota(jnp.int32, shape, 1) % count)
-    read = jnp.dot(maps[count:].T.astype(BF16), spread.astype(BF16), preferred_element_type=F32)
-    held_at = lax.broadcasted_iota(jnp.int32, read.shape, 1) // count
-    own = held_at == lax.broadcasted_iota(jnp.int32, read.shape, 0) % span
-    read_ref[...] = jnp.where(own, read, 0.0).astype(BF16)
+    spread_entry(maps_ref, entry_ref)
     state = jnp.concatenate(
         [
             jnp.concatenate([enter_ref[2 * block], enter_ref[2 * block + 1]], axis=0)
@@ -255,12 +260,6 @@
         (mamba_in, halo, conv_weight[0], conv_bias, state_weight.T),
         nbytes=4 << 20,
     )
-    queries, _ = lax.optimization_barrier((queries, act))
-    grouped = queries.reshape(rows, kv_heads, group, width)
-    own_q = lax.dynamic_index_in_dim(grouped, zc, 1, False)
-    other_q = lax.ppermute(lax.dynamic_index_in_dim(grouped, 1 - zc, 1, False), "zc", swap)
-    place = jnp.stack([zh, zc, core]).astype(jnp.int32)
-
     step = kernel_call(
         step_body,
         jax.ShapeDtypeStruct((rows, cols), F32),
@@ -269,6 +268,12 @@
         nbytes=4 << 20,
     )
     maps = lax.all_to_all(partial, "tp", 0, 0, tiled=True)
+    queries, maps = lax.optimization_barrier((queries, maps))
+    grouped = queries.reshape(rows, kv_heads, group, width)
+    own_q = lax.dynamic_index_in_dim(grouped, zc, 1, False)
+    other_q = lax.ppermute(lax.dynamic_index_in_dim(grouped, 1 - zc, 1, False), "zc", swap)
+    place = jnp.stack([zh, zc, core]).astype(jnp.int32)
+
     span = 32
     parts = kernel_call(
         local_body,
@@ -279,7 +284,13 @@
     )
     parts = lax.all_to_all(parts, CTX, 0, 0, tiled=True)
     entering = kernel_call(
-        prefix_body, jax.ShapeDtypeStruct((places, count // 2, 128), F32), (parts, other_q), nbytes=1 << 20
+        prefix_body, jax.ShapeDtypeStruct((places, count // 2, 128), F32), (parts,), nbytes=1 << 20
+    )
+    read = kernel_call(
+        read_body,
+        jax.ShapeDtypeStruct((rows, span * count), BF16),
+        (maps, entering, other_q),
+        nbytes=1 << 20,
     )
     entering = lax.all_to_all(entering, CTX, 0, 0, tiled=True)
     def attend(q, slot, after):
@@ -302,12 +313,11 @@
     gated = kernel_call(
         scan_body,
         jax.ShapeDtypeStruct((rows, cols), BF16),
-        (step, act, maps, decay_rate, entering, skip_gain, gate_in),
+        (step, act, maps, read, decay_rate, entering, skip_gain, gate_in),
 
         scratch=[
             pltpu.VMEM((rows, cols), F32),
             pltpu.VMEM((rows, count, 128), F32),
-            pltpu.VMEM((rows, span * count), BF16),
             pltpu.VMEM((span * count, cols), BF16),
         ],
         nbytes=16 << 20,

time: 133 us -> 127 us (0.955)
  starting transfers between devices: 46.5 us -> 40.4 us
    all_to_all x1, starting transfers between devices: 11.8 us -> 5 us  [per_device(): entering = lax.all_to_all(entering, CTX, 0, 0, tiled=True)]
    ppermute x1, waiting for transfers between devices: 11 us -> 6.54 us  [per_device(): lax.ppermute(lax.dynamic_index_in_dim(grouped, 1 - zc, 1, False), 'zc', s...]
    all_to_all x1, waiting for transfers between devices: 0.16 us -> 3.3 us  [per_device(): entering = lax.all_to_all(entering, CTX, 0, 0, tiled=True)]
    pallas_call x7 -> x8, Pallas kernels: 12.9 us -> 13.9 us  [kernel_call(): pl.pallas_call(body, out_shape=out_shape, in_specs=specs or [VMEM] * len(...]
  transfers between devices with their start and end apart: 9 -> 9, of which waited for: 6 -> 6; matrix products, arithmetic and copies ran while one was open for 1% -> 1% of each run, Pallas kernels for 10% -> 11%
where the time goes in v3:
time: 127 us; the launch traced here: 126 us
  starting transfers between devices  40.4 us (32%)
  blocking collectives  25.8 us (20%)
  waiting for transfers between devices  21 us (17%)
  between operations  14.3 us (11%)
  Pallas kernels  13.9 us (11%)
  local copies, waits for them, and re-layouts  9.56 us (8%)
  other arithmetic  1.61 us (1%)
    all_to_all x1, blocking collectives, per_device(): parts = lax.all_to_all(parts, CTX, 0, 0, tiled=True)  25.8 us
    ppermute x1, starting transfers between devices, per_device(): lax.ppermute(mamba_in[rows - HALO:], CTX, [(i, i + 1) for i in range(plac...  14.8 us
    pallas_call x8, Pallas kernels, kernel_call(): pl.pallas_call(body, out_shape=out_shape, in_specs=specs or [VMEM] * len(...  13.9 us
    unnamed x27, local copies, waits for them, and re-layouts  7.35 us
    ppermute x1, waiting for transfers between devices, per_device(): lax.ppermute(lax.dynamic_index_in_dim(grouped, 1 - zc, 1, False), 'zc', s...  6.54 us
    ppermute x1, waiting for transfers between devices, per_device(): lax.ppermute(gated, 'pipe', [(i, (i + 1) % pipes) for i in range(pipes)])  5.28 us
    all_to_all x1, starting transfers between devices, per_device(): entering = lax.all_to_all(entering, CTX, 0, 0, tiled=True)  5 us
    ppermute x1, starting transfers between devices, per_device(): lax.ppermute(lax.dynamic_index_in_dim(key_value, 1 - zc, 2, False), 'zc',...  4.83 us
  transfers between devices with their start and end apart: 9, of which 6 were waited for; matrix products, arithmetic and copies ran while one was open for 1% of the time, Pallas kernels for 11%

profile of v3, /device:TPU:1, one launch (start us, length us, event | category | flops | bytes accessed | tf_op | source)
XLA Modules:
  0.0 126.5 jit_solution(139862719789953282)
XLA Ops:
  7.2 0.0 copy-start.4
  7.2 0.0 copy-start.8
  7.2 0.0 all-gather.3.cloned.1.call-start
  7.2 1.3 constant_dynamic-slice_fusion.1
  8.5 4.8 %collective-permute-start = (bf16[2,128,128]{2,1,0:T(8,128)(2,1)S(1)}, bf16[2,128,128]{2,1,0:T(8,128)(2,1)S(1)}, u32[]{:S(2)}, u32[]{:S(2)}) collective-permute-start(bf16[2,128,128]{2,1,0:T(8,128)(2,1)S(1)} %bitcast.63), channel_id=1, source_target_pairs={{0,8},{8,0},{1,9},{9,1},{2,10},{10,2},{3,11},{11,3},{4,12},{12,4},... | collective-permute-start | bytes 196616 | tf_op jit(solution)/shard_map/ppermute | solution.py:251
  13.4 0.8 slice_bitcast_fusion
  14.2 14.8 %collective-permute-start.1 = (bf16[16,2048]{1,0:T(8,128)(2,1)S(1)}, bf16[16,2048]{1,0:T(8,128)(2,1)S(1)}, u32[]{:S(2)}, u32[]{:S(2)}) collective-permute-start(bf16[16,2048]{1,0:T(8,128)(2,1)S(1)} %slice_bitcast_fusion), channel_id=1, source_target_pairs={{0,4},{4,8},{8,12},{12,16},{16,20},{20,24},{24,28},{28,32},{32,36}... | collective-permute-start | bytes 196616 | tf_op jit(solution)/shard_map/ppermute | solution.py:252
  29.0 0.0 collective-permute-done
  29.0 1.3 %collective-permute-done.1.halo_ref = bf16[16,2048]{1,0:T(8,128)(2,1)S(1)} collective-permute-done((bf16[16,2048]{1,0:T(8,128)(2,1)S(1)}, bf16[16,2048]{1,0:T(8,128)(2,1)S(1)}, u32[]{:S(2)}, u32[]{:S(2)}) %collective-permute-start.1) | collective-permute-done | bytes 65568 | tf_op jit(solution)/shard_map/ppermute | solution.py:252
  30.3 0.7 pad_maximum_fusion
  31.0 0.0 all-gather.3.cloned.1.call-update
  31.0 0.0 copy-start.1
  31.0 1.0 copy-done.1
  32.0 0.8 copy-done.5
  32.9 0.8 copy-done.6
  33.6 0.7 copy-done.7
  34.3 1.8 %shard_map.131 = (bf16[128,2048]{1,0:T(8,128)(2,1)S(1)}, f32[4,16,128]{2,1,0:T(8,128)}) custom-call(bf16[128,2048]{1,0:T(8,128)(2,1)S(1)} %bitcast.43, bf16[16,2048]{1,0:T(8,128)(2,1)S(1)} %collective-permute-done.1.halo_ref, f32[4,2048]{1,0:T(4,128)S(1)} %bitcast.51, f32[1,2048]{1,0:T(1,128)S(1)} %copy-done.7, bf16[16,2048]{1,0:T(8,128)(2,1)S(1)} %bitcast.50), custom_call_target="tpu_custom_call" | custom-call | bytes 4194304 | tf_op jit(solution)/shard_map/pallas_call | solution.py:22
  36.1 3.4 %all-to-all-start = ((f32[4,16,128]{2,1,0:T(8,128)}), f32[4,16,128]{2,1,0:T(8,128)S(1)}, u32[]{:S(2)}, u32[]{:S(2)}) async-start(f32[4,16,128]{2,1,0:T(8,128)} %get-tuple-element.10), calls=%async_computation | async-start | bytes 65536 | tf_op jit(solution)/shard_map/all_to_all | solution.py:270
  39.5 0.0 copy-done.4
  39.6 0.0 copy-done.8
  39.6 0.0 copy-start
  39.6 1.6 %copy-done = bf16[1,512,2048]{2,1,0:T(8,128)(2,1)S(1)} copy-done((bf16[1,512,2048]{2,1,0:T(8,128)(2,1)S(1)}, bf16[1,512,2048]{2,1,0:T(8,128)(2,1)}, u32[]{:S(2)}) %copy-start) | copy-done | bytes 2097176
  41.2 0.9 shard_map.132.step_ref
  42.0 0.0 copy-start.2
  42.0 0.0 copy-start.9
  42.0 1.8 %all-to-all-done.maps_ref = f32[4,16,128]{2,1,0:T(8,128)S(1)} async-done(((f32[4,16,128]{2,1,0:T(8,128)}), f32[4,16,128]{2,1,0:T(8,128)S(1)}, u32[]{:S(2)}, u32[]{:S(2)}) %all-to-all-start) | async-done | bytes 32800 | tf_op jit(solution)/shard_map/all_to_all | solution.py:270
  43.8 3.4 %shard_map.133 = bf16[32,8,128]{2,1,0:T(8,128)(2,1)S(1)} custom-call(f32[128,2048]{1,0:T(8,128)S(1)} %shard_map.132.step_ref, bf16[128,2048]{1,0:T(8,128)(2,1)S(1)} %get-tuple-element.14.after_ref.act_ref, f32[4,16,128]{2,1,0:T(8,128)S(1)} %all-to-all-done.maps_ref, f32[8,2048]{1,0:T(8,128)S(1)} %bitcast.45), custom_call_target="tpu_custom_call" | custom-call | bytes 16777216 | tf_op jit(solution)/shard_map/pallas_call | solution.py:22
  47.2 25.8 %all_to_all.15.in_ref = bf16[32,8,128]{2,1,0:T(8,128)(2,1)S(1)} all-to-all(bf16[32,8,128]{2,1,0:T(8,128)(2,1)S(1)} %shard_map.133), channel_id=1, replica_groups=mesh['pipe'=8,'zh'=8,'zc'=2,'core'=2,'tp'=4] {'zh','zc','core'}, dimensions={0} | all-to-all | bytes 131072 | tf_op jit(solution)/shard_map/all_to_all | solution.py:285
  73.0 0.7 shard_map.134.asked_ref
  73.7 5.0 %all-to-all-start.2 = ((f32[32,4,128]{2,1,0:T(4,128)}), f32[32,4,128]{2,1,0:T(4,128)S(1)}, u32[]{:S(2)}, u32[]{:S(2)}) async-start(f32[32,4,128]{2,1,0:T(4,128)} %shard_map.134.asked_ref), calls=%async_computation.2 | async-start | bytes 131072 | tf_op jit(solution)/shard_map/all_to_all | solution.py:295
  78.7 0.1 constant_dynamic-slice_fusion
  78.8 3.3 %collective-permute-start.2 = (bf16[128,4,128]{2,1,0:T(4,128)(2,1)S(1)}, bf16[128,4,128]{2,1,0:T(4,128)(2,1)S(1)}, u32[]{:S(2)}, u32[]{:S(2)}) collective-permute-start(bf16[128,4,128]{2,1,0:T(4,128)(2,1)S(1)} %get-tuple-element.19), channel_id=1, source_target_pairs={{0,8},{8,0},{1,9},{9,1},{2,10},{10,2},{3,11},{11,3},{4,12},{12,4},... | collective-permute-start | bytes 393224 | tf_op jit(solution)/shard_map/ppermute | solution.py:274
  82.1 6.5 %collective-permute-done.2.after_ref = bf16[128,4,128]{2,1,0:T(4,128)(2,1)S(1)} collective-permute-done((bf16[128,4,128]{2,1,0:T(4,128)(2,1)S(1)}, bf16[128,4,128]{2,1,0:T(4,128)(2,1)S(1)}, u32[]{:S(2)}, u32[]{:S(2)}) %collective-permute-start.2) | collective-permute-done | bytes 131104 | tf_op jit(solution)/shard_map/ppermute | solution.py:274
  88.7 1.1 shard_map.135.read_ref
  89.7 3.3 %all-to-all-done.2.enter_ref = f32[32,4,128]{2,1,0:T(4,128)S(1)} async-done(((f32[32,4,128]{2,1,0:T(4,128)}), f32[32,4,128]{2,1,0:T(4,128)S(1)}, u32[]{:S(2)}, u32[]{:S(2)}) %all-to-all-start.2) | async-done | bytes 65568 | tf_op jit(solution)/shard_map/all_to_all | solution.py:295
  93.1 3.4 %shard_map.136.after_ref = bf16[128,2048]{1,0:T(8,128)(2,1)S(1)} custom-call(f32[128,2048]{1,0:T(8,128)S(1)} %shard_map.132.step_ref, bf16[128,2048]{1,0:T(8,128)(2,1)S(1)} %get-tuple-element.14.after_ref.act_ref, f32[4,16,128]{2,1,0:T(8,128)S(1)} %all-to-all-done.maps_ref, bf16[128,256]{1,0:T(8,128)(2,1)S(1)} %shard_map.135.read_ref, ...), custom_call_target="tpu_custom_call" | custom-call | bytes 16777216 | tf_op jit(solution)/shard_map/pallas_call | solution.py:22
  96.4 2.7 %collective-permute-start.5 = (bf16[128,2048]{1,0:T(8,128)(2,1)S(1)}, bf16[128,2048]{1,0:T(8,128)(2,1)S(1)}, u32[]{:S(2)}, u32[]{:S(2)}) collective-permute-start(bf16[128,2048]{1,0:T(8,128)(2,1)S(1)} %shard_map.136.after_ref), channel_id=1, source_target_pairs={{0,128},{128,256},{256,384},{384,512},{512,640},{640,768},{768,896... | collective-permute-start | bytes 1572872 | tf_op jit(solution)/shard_map/ppermute | solution.py:325
  99.1 0.1 pad_add_fusion.place_ref
  99.2 1.6 %copy-done.10 = bf16[32,2,128,128]{3,2,1,0:T(8,128)(2,1)S(1)} copy-done((bf16[32,2,128,128]{3,2,1,0:T(8,128)(2,1)S(1)}, bf16[32,2,128,128]{3,2,1,0:T(8,128)(2,1)}, u32[]{:S(2)}) %copy-start.10) | copy-done | bytes 2097176
  100.8 1.3 %shard_map.138 = bf16[512,128]{1,0:T(8,128)(2,1)S(1)} custom-call(s32[3]{0:T(128)S(1)} %pad_add_fusion.place_ref, bf16[512,128]{1,0:T(8,128)(2,1)S(1)} %bitcast.47, bf16[8,2,2,2,128,128]{5,4,3,2,1,0:T(8,128)(2,1)S(1)} %bitcast.52, bf16[128,2048]{1,0:T(8,128)(2,1)S(1)} %shard_map.136.after_ref), custom_call_target="tpu_custom_call" | custom-call | flops 1073741824 | bytes 16777216 | tf_op jit(solution)/shard_map/pallas_call | solution.py:22
  102.1 3.4 %collective-permute-start.4 = (bf16[128,4,128]{2,1,0:T(4,128)(2,1)S(1)}, bf16[128,4,128]{2,1,0:T(4,128)(2,1)S(1)}, u32[]{:S(2)}, u32[]{:S(2)}) collective-permute-start(bf16[128,4,128]{2,1,0:T(4,128)(2,1)S(1)} %bitcast.54), channel_id=1, source_target_pairs={{0,136},{8,128},{128,264},{136,256},{256,392},{264,384},{384,520},... | collective-permute-start | bytes 393224 | tf_op jit(solution)/shard_map/ppermute | solution.py:327
  105.5 1.4 %shard_map.137 = bf16[512,128]{1,0:T(8,128)(2,1)S(1)} custom-call(s32[3]{0:T(128)S(1)} %pad_add_fusion.place_ref, bf16[512,128]{1,0:T(8,128)(2,1)S(1)} %bitcast.48, bf16[8,2,2,2,128,128]{5,4,3,2,1,0:T(8,128)(2,1)S(1)} %bitcast.53, bf16[128,2048]{1,0:T(8,128)(2,1)S(1)} %shard_map.136.after_ref), custom_call_target="tpu_custom_call" | custom-call | flops 1073741824 | bytes 16777216 | tf_op jit(solution)/shard_map/pallas_call | solution.py:22
  106.8 3.0 %collective-permute-start.3 = (bf16[128,4,128]{2,1,0:T(4,128)(2,1)S(1)}, bf16[128,4,128]{2,1,0:T(4,128)(2,1)S(1)}, u32[]{:S(2)}, u32[]{:S(2)}) collective-permute-start(bf16[128,4,128]{2,1,0:T(4,128)(2,1)S(1)} %bitcast.55), channel_id=1, source_target_pairs={{0,128},{128,256},{256,384},{384,512},{512,640},{640,768},{768,896... | collective-permute-start | bytes 393224 | tf_op jit(solution)/shard_map/ppermute | solution.py:333
  109.9 5.3 %collective-permute-done.5 = bf16[128,2048]{1,0:T(8,128)(2,1)S(1)} collective-permute-done((bf16[128,2048]{1,0:T(8,128)(2,1)S(1)}, bf16[128,2048]{1,0:T(8,128)(2,1)S(1)}, u32[]{:S(2)}, u32[]{:S(2)}) %collective-permute-start.5) | collective-permute-done | bytes 524320 | tf_op jit(solution)/shard_map/ppermute | solution.py:325
  115.2 0.0 collective-permute-done.4
  115.2 2.8 %collective-permute-done.3 = bf16[128,4,128]{2,1,0:T(4,128)(2,1)S(1)} collective-permute-done((bf16[128,4,128]{2,1,0:T(4,128)(2,1)S(1)}, bf16[128,4,128]{2,1,0:T(4,128)(2,1)S(1)}, u32[]{:S(2)}, u32[]{:S(2)}) %collective-permute-start.3) | collective-permute-done | bytes 131104 | tf_op jit(solution)/shard_map/ppermute | solution.py:333
  118.0 0.8 maximum_bitcast_fusion
  118.9 0.8 copy.33
  (14 shorter events, 0.1 us)
Async XLA Ops:
  7.2 32.4 %copy-start.4 = (bf16[1,128,512]{2,1,0:T(8,128)(2,1)S(1)}, bf16[1,128,512]{2,1,0:T(8,128)(2,1)}, u32[]{:S(2)}) copy-start(bf16[1,128,512]{2,1,0:T(8,128)(2,1)} %param.16) | copy-start | bytes 393220
  7.2 32.4 %copy-start.8 = (f32[1,2048]{1,0:T(1,128)S(1)}, f32[1,2048]{1,0:T(1,128)}, u32[]{:S(2)}) copy-start(f32[1,2048]{1,0:T(1,128)} %bias_ref.3) | copy-start | bytes 24580
  7.2 92.0 %all-gather.3.cloned.1.call-start = ((), (), s32[]{:S(2)}) async-start(), calls=%async_computation.3 | async-start | bytes 2228224 | tf_op jit(solution)/shard_map/all_gather | solution.py:254
  8.5 20.5 %collective-permute-start = (bf16[2,128,128]{2,1,0:T(8,128)(2,1)S(1)}, bf16[2,128,128]{2,1,0:T(8,128)(2,1)S(1)}, u32[]{:S(2)}, u32[]{:S(2)}) collective-permute-start(bf16[2,128,128]{2,1,0:T(8,128)(2,1)S(1)} %bitcast.63), channel_id=1, source_target_pairs={{0,8},{8,0},{1,9},{9,1},{2,10},{10,2},{3,11},{11,3},{4,12},{12,4},... | collective-permute-start | bytes 196616 | tf_op jit(solution)/shard_map/ppermute | solution.py:251
  14.2 16.1 %collective-permute-start.1 = (bf16[16,2048]{1,0:T(8,128)(2,1)S(1)}, bf16[16,2048]{1,0:T(8,128)(2,1)S(1)}, u32[]{:S(2)}, u32[]{:S(2)}) collective-permute-start(bf16[16,2048]{1,0:T(8,128)(2,1)S(1)} %slice_bitcast_fusion), channel_id=1, source_target_pairs={{0,4},{4,8},{8,12},{12,16},{16,20},{20,24},{24,28},{28,32},{32,36}... | collective-permute-start | bytes 196616 | tf_op jit(solution)/shard_map/ppermute | solution.py:252
  31.0 1.0 copy-start.1
  32.0 0.8 copy-start.5
  32.9 0.8 copy-start.6
  33.6 0.7 copy-start.7
  36.1 7.7 %copy-start.3 = (f32[1,8,2048]{2,1,0:T(8,128)S(1)}, f32[1,8,2048]{2,1,0:T(8,128)}, u32[]{:S(2)}) copy-start(f32[1,8,2048]{2,1,0:T(8,128)} %param.19) | copy-start | bytes 196612
  36.1 7.7 %all-to-all-start = ((f32[4,16,128]{2,1,0:T(8,128)}), f32[4,16,128]{2,1,0:T(8,128)S(1)}, u32[]{:S(2)}, u32[]{:S(2)}) async-start(f32[4,16,128]{2,1,0:T(8,128)} %get-tuple-element.10), calls=%async_computation | async-start | bytes 65536 | tf_op jit(solution)/shard_map/all_to_all | solution.py:270
  39.6 1.6 %copy-start = (bf16[1,512,2048]{2,1,0:T(8,128)(2,1)S(1)}, bf16[1,512,2048]{2,1,0:T(8,128)(2,1)}, u32[]{:S(2)}) copy-start(bf16[1,512,2048]{2,1,0:T(8,128)(2,1)} %param.17) | copy-start | bytes 6291460
  41.2 37.6 %copy-start.11 = (bf16[1,128,8,128]{3,2,1,0:T(8,128)(2,1)S(1)}, bf16[1,128,8,128]{3,2,1,0:T(8,128)(2,1)}, u32[]{:S(2)}) copy-start(bf16[1,128,8,128]{3,2,1,0:T(8,128)(2,1)} %param.12) | copy-start | bytes 786436
  42.0 51.0 %copy-start.2 = (bf16[1,128,2048]{2,1,0:T(8,128)(2,1)S(1)}, bf16[1,128,2048]{2,1,0:T(8,128)(2,1)}, u32[]{:S(2)}) copy-start(bf16[1,128,2048]{2,1,0:T(8,128)(2,1)} %param.15) | copy-start | bytes 1572868
  42.0 51.0 %copy-start.9 = (f32[1,2048]{1,0:T(1,128)S(1)}, f32[1,2048]{1,0:T(1,128)}, u32[]{:S(2)}) copy-start(f32[1,2048]{1,0:T(1,128)} %skip_ref.1) | copy-start | bytes 24580
  73.7 19.3 %all-to-all-start.2 = ((f32[32,4,128]{2,1,0:T(4,128)}), f32[32,4,128]{2,1,0:T(4,128)S(1)}, u32[]{:S(2)}, u32[]{:S(2)}) async-start(f32[32,4,128]{2,1,0:T(4,128)} %shard_map.134.asked_ref), calls=%async_computation.2 | async-start | bytes 131072 | tf_op jit(solution)/shard_map/all_to_all | solution.py:295
  78.8 9.8 %collective-permute-start.2 = (bf16[128,4,128]{2,1,0:T(4,128)(2,1)S(1)}, bf16[128,4,128]{2,1,0:T(4,128)(2,1)S(1)}, u32[]{:S(2)}, u32[]{:S(2)}) collective-permute-start(bf16[128,4,128]{2,1,0:T(4,128)(2,1)S(1)} %get-tuple-element.19), channel_id=1, source_target_pairs={{0,8},{8,0},{1,9},{9,1},{2,10},{10,2},{3,11},{11,3},{4,12},{12,4},... | collective-permute-start | bytes 393224 | tf_op jit(solution)/shard_map/ppermute | solution.py:274
  96.4 18.8 %collective-permute-start.5 = (bf16[128,2048]{1,0:T(8,128)(2,1)S(1)}, bf16[128,2048]{1,0:T(8,128)(2,1)S(1)}, u32[]{:S(2)}, u32[]{:S(2)}) collective-permute-start(bf16[128,2048]{1,0:T(8,128)(2,1)S(1)} %shard_map.136.after_ref), channel_id=1, source_target_pairs={{0,128},{128,256},{256,384},{384,512},{512,640},{640,768},{768,896... | collective-permute-start | bytes 1572872 | tf_op jit(solution)/shard_map/ppermute | solution.py:325
  99.2 1.6 %copy-start.10 = (bf16[32,2,128,128]{3,2,1,0:T(8,128)(2,1)S(1)}, bf16[32,2,128,128]{3,2,1,0:T(8,128)(2,1)}, u32[]{:S(2)}) copy-start(bf16[32,2,128,128]{3,2,1,0:T(8,128)(2,1)} %all-gather.3.cloned.1.call-done) | copy-start | bytes 6291460
  102.1 13.1 %collective-permute-start.4 = (bf16[128,4,128]{2,1,0:T(4,128)(2,1)S(1)}, bf16[128,4,128]{2,1,0:T(4,128)(2,1)S(1)}, u32[]{:S(2)}, u32[]{:S(2)}) collective-permute-start(bf16[128,4,128]{2,1,0:T(4,128)(2,1)S(1)} %bitcast.54), channel_id=1, source_target_pairs={{0,136},{8,128},{128,264},{136,256},{256,392},{264,384},{384,520},... | collective-permute-start | bytes 393224 | tf_op jit(solution)/shard_map/ppermute | solution.py:327
  106.8 11.1 %collective-permute-start.3 = (bf16[128,4,128]{2,1,0:T(4,128)(2,1)S(1)}, bf16[128,4,128]{2,1,0:T(4,128)(2,1)S(1)}, u32[]{:S(2)}, u32[]{:S(2)}) collective-permute-start(bf16[128,4,128]{2,1,0:T(4,128)(2,1)S(1)} %bitcast.55), channel_id=1, source_target_pairs={{0,128},{128,256},{256,384},{384,512},{512,640},{640,768},{768,896... | collective-permute-start | bytes 393224 | tf_op jit(solution)/shard_map/ppermute | solution.py:333
Sparse Core Ops, SparseCore 0:
  31.1 57.7 all-gather.2

commit v4 on v3

--- a/solution.py
+++ b/solution.py
@@ -123,7 +123,7 @@
 
 
 def scan_body(
-    step_ref, act_ref, maps_ref, read_ref, rate_ref, enter_ref, skip_ref, gate_ref, out_ref,
+    step_ref, act_ref, maps_ref, read_ref, rate_ref, enter_ref, skip_ref, gate_ref, after_ref, out_ref,
     drive_ref, entry_ref, held_ref,
 ):
     rows, cols = step_ref.shape
@@ -283,16 +283,16 @@
         nbytes=16 << 20,
     )
     parts = lax.all_to_all(parts, CTX, 0, 0, tiled=True)
-    entering = kernel_call(
+    asked = kernel_call(
         prefix_body, jax.ShapeDtypeStruct((places, count // 2, 128), F32), (parts,), nbytes=1 << 20
     )
     read = kernel_call(
         read_body,
         jax.ShapeDtypeStruct((rows, span * count), BF16),
-        (maps, entering, other_q),
+        (maps, asked, other_q),
         nbytes=1 << 20,
     )
-    entering = lax.all_to_all(entering, CTX, 0, 0, tiled=True)
+    entering = lax.all_to_all(asked, CTX, 0, 0, tiled=True)
     def attend(q, slot, after):
         lines = rows * group
         keys = 4 * rows
@@ -310,10 +310,16 @@
             nbytes=16 << 20,
         ).reshape(rows, group, width)
 
+    far = attend(other_q, 1, asked)
+    far_sent = lax.ppermute(
+        far,
+        ("pipe", "zc"),
+        [(2 * i + j, 2 * ((i + 1) % pipes) + 1 - j) for i in range(pipes) for j in range(2)],
+    )
     gated = kernel_call(
         scan_body,
         jax.ShapeDtypeStruct((rows, cols), BF16),
-        (step, act, maps, read, decay_rate, entering, skip_gain, gate_in),
+        (step, act, maps, read, decay_rate, entering, skip_gain, gate_in, far),
 
         scratch=[
             pltpu.VMEM((rows, cols), F32),
@@ -323,13 +329,7 @@
         nbytes=16 << 20,
     )
     mamba_out = lax.ppermute(gated, "pipe", [(i, (i + 1) % pipes) for i in range(pipes)])
-    far = attend(other_q, 1, gated)
-    far_sent = lax.ppermute(
-        far,
-        ("pipe", "zc"),
-        [(2 * i + j, 2 * ((i + 1) % pipes) + 1 - j) for i in range(pipes) for j in range(2)],
-    )
-    near = attend(own_q, 0, gated)
+    near = attend(own_q, 0, far_sent)
     near = lax.ppermute(near, "pipe", [(i, (i + 1) % pipes) for i in range(pipes)])
     far = far_sent
     first = jnp.where(zc == 0, near, far)

time: 127 us -> 130 us (1.024)
  blocking collectives: 25.8 us -> 0 us
  waiting for transfers between devices: 21 us -> 35.3 us
  starting transfers between devices: 40.4 us -> 52.7 us
    all_to_all x1 -> x0, blocking collectives: 25.8 us -> none  [per_device(): parts = lax.all_to_all(parts, CTX, 0, 0, tiled=True)]
    all_to_all x1 -> x2, starting transfers between devices: 5 us -> 16.5 us  [the longest x1 11.8 us: per_device(): parts = lax.all_to_all(parts, CTX, 0, 0, tiled=True)]
    all_gather x1, waiting for transfers between devices: 0.01 us -> 9.29 us  [per_device(): kv = lax.all_gather(jnp.stack([own_kv, other_kv]), ('zh', 'core'))]
    all_to_all x1 -> x2, waiting for transfers between devices: 3.3 us -> 11.8 us  [the longest x1 11.8 us: per_device(): parts = lax.all_to_all(parts, CTX, 0, 0, tiled=True)]
    ppermute x1, waiting for transfers between devices: 2.81 us -> 11.1 us  [per_device(): lax.ppermute(near, 'pipe', [(i, (i + 1) % pipes) for i in range(pipes)])]
    ppermute x1, waiting for transfers between devices: 6.54 us -> 0.01 us  [per_device(): lax.ppermute(lax.dynamic_index_in_dim(grouped, 1 - zc, 1, False), 'zc', s...]
    ppermute x1, waiting for transfers between devices: 5.28 us -> 0.01 us  [per_device(): lax.ppermute(gated, 'pipe', [(i, (i + 1) % pipes) for i in range(pipes)])]
    unnamed x27 -> x29, local copies, waits for them, and re-layouts: 7.35 us -> 7.35 us
  transfers between devices with their start and end apart: 9 -> 10, of which waited for: 6 -> 5; matrix products, arithmetic and copies ran while one was open for 1% -> 1% of each run, Pallas kernels for 11% -> 12%
where the time goes in v4:
time: 130 us; the launch traced here: 128 us
  starting transfers between devices  52.7 us (41%)
  waiting for transfers between devices  35.3 us (27%)
  Pallas kernels  14.9 us (11%)
  between operations  14.3 us (11%)
  local copies, waits for them, and re-layouts  9.56 us (7%)
  other arithmetic  1.61 us (1%)
    pallas_call x8, Pallas kernels, kernel_call(): pl.pallas_call(body, out_shape=out_shape, in_specs=specs or [VMEM] * len(...  14.9 us
    ppermute x1, starting transfers between devices, per_device(): lax.ppermute(mamba_in[rows - HALO:], CTX, [(i, i + 1) for i in range(plac...  14.8 us
    all_to_all x1, starting transfers between devices, per_device(): parts = lax.all_to_all(parts, CTX, 0, 0, tiled=True)  11.8 us
    all_to_all x1, waiting for transfers between devices, per_device(): parts = lax.all_to_all(parts, CTX, 0, 0, tiled=True)  11.8 us
    ppermute x1, waiting for transfers between devices, per_device(): lax.ppermute(near, 'pipe', [(i, (i + 1) % pipes) for i in range(pipes)])  11.1 us
    all_gather x1, waiting for transfers between devices, per_device(): kv = lax.all_gather(jnp.stack([own_kv, other_kv]), ('zh', 'core'))  9.29 us
    unnamed x29, local copies, waits for them, and re-layouts  7.35 us
    ppermute x1, starting transfers between devices, per_device(): lax.ppermute(lax.dynamic_index_in_dim(key_value, 1 - zc, 2, False), 'zc',...  4.83 us
  transfers between devices with their start and end apart: 10, of which 5 were waited for; matrix products, arithmetic and copies ran while one was open for 1% of the time, Pallas kernels for 12%

profile of v4, /device:TPU:1, one launch (start us, length us, event | category | flops | bytes accessed | tf_op | source)
XLA Modules:
  0.0 128.3 jit_solution(5890638693317948811)
XLA Ops:
  7.2 0.0 copy-start.4
  7.2 0.0 copy-start.8
  7.2 0.0 all-gather.3.cloned.1.call-start
  7.2 1.3 constant_dynamic-slice_fusion.1
  8.5 4.8 %collective-permute-start = (bf16[2,128,128]{2,1,0:T(8,128)(2,1)S(1)}, bf16[2,128,128]{2,1,0:T(8,128)(2,1)S(1)}, u32[]{:S(2)}, u32[]{:S(2)}) collective-permute-start(bf16[2,128,128]{2,1,0:T(8,128)(2,1)S(1)} %bitcast.64), channel_id=1, source_target_pairs={{0,8},{8,0},{1,9},{9,1},{2,10},{10,2},{3,11},{11,3},{4,12},{12,4},... | collective-permute-start | bytes 196616 | tf_op jit(solution)/shard_map/ppermute | solution.py:251
  13.4 0.8 slice_bitcast_fusion
  14.2 14.8 %collective-permute-start.1 = (bf16[16,2048]{1,0:T(8,128)(2,1)S(1)}, bf16[16,2048]{1,0:T(8,128)(2,1)S(1)}, u32[]{:S(2)}, u32[]{:S(2)}) collective-permute-start(bf16[16,2048]{1,0:T(8,128)(2,1)S(1)} %slice_bitcast_fusion), channel_id=1, source_target_pairs={{0,4},{4,8},{8,12},{12,16},{16,20},{20,24},{24,28},{28,32},{32,36}... | collective-permute-start | bytes 196616 | tf_op jit(solution)/shard_map/ppermute | solution.py:252
  29.0 0.0 collective-permute-done
  29.0 1.3 collective-permute-done.1.halo_ref
  30.3 0.7 pad_maximum_fusion
  31.0 0.0 all-gather.3.cloned.1.call-update
  31.0 0.0 copy-start.1
  31.0 1.0 copy-done.1
  32.0 0.8 copy-done.5
  32.9 0.8 copy-done.6
  33.6 0.7 copy-done.7
  34.3 1.8 %shard_map.131 = (bf16[128,2048]{1,0:T(8,128)(2,1)S(1)}, f32[4,16,128]{2,1,0:T(8,128)}) custom-call(bf16[128,2048]{1,0:T(8,128)(2,1)S(1)} %bitcast.43, bf16[16,2048]{1,0:T(8,128)(2,1)S(1)} %collective-permute-done.1.halo_ref, f32[4,2048]{1,0:T(4,128)S(1)} %bitcast.54, f32[1,2048]{1,0:T(1,128)S(1)} %copy-done.7, bf16[16,2048]{1,0:T(8,128)(2,1)S(1)} %bitcast.53), custom_call_target="tpu_custom_call" | custom-call | bytes 4194304 | tf_op jit(solution)/shard_map/pallas_call | solution.py:22
  36.1 3.4 %all-to-all-start = ((f32[4,16,128]{2,1,0:T(8,128)}), f32[4,16,128]{2,1,0:T(8,128)S(1)}, u32[]{:S(2)}, u32[]{:S(2)}) async-start(f32[4,16,128]{2,1,0:T(8,128)} %get-tuple-element.10), calls=%async_computation | async-start | bytes 65536 | tf_op jit(solution)/shard_map/all_to_all | solution.py:270
  39.5 0.0 copy-done.4
  39.6 0.0 copy-start
  39.6 1.6 %copy-done = bf16[1,512,2048]{2,1,0:T(8,128)(2,1)S(1)} copy-done((bf16[1,512,2048]{2,1,0:T(8,128)(2,1)S(1)}, bf16[1,512,2048]{2,1,0:T(8,128)(2,1)}, u32[]{:S(2)}) %copy-start) | copy-done | bytes 2097176
  41.2 0.9 shard_map.132.step_ref
  42.0 1.8 %all-to-all-done.maps_ref = f32[4,16,128]{2,1,0:T(8,128)S(1)} async-done(((f32[4,16,128]{2,1,0:T(8,128)}), f32[4,16,128]{2,1,0:T(8,128)S(1)}, u32[]{:S(2)}, u32[]{:S(2)}) %all-to-all-start) | async-done | bytes 32800 | tf_op jit(solution)/shard_map/all_to_all | solution.py:270
  43.8 4.0 %shard_map.133 = bf16[32,8,128]{2,1,0:T(8,128)(2,1)} custom-call(f32[128,2048]{1,0:T(8,128)S(1)} %shard_map.132.step_ref, bf16[128,2048]{1,0:T(8,128)(2,1)S(1)} %get-tuple-element.14.after_ref.act_ref, f32[4,16,128]{2,1,0:T(8,128)S(1)} %all-to-all-done.maps_ref, f32[8,2048]{1,0:T(8,128)S(1)} %bitcast.45), custom_call_target="tpu_custom_call" | custom-call | bytes 16777216 | tf_op jit(solution)/shard_map/pallas_call | solution.py:22
  47.8 11.8 %all-to-all-start.1 = ((bf16[32,8,128]{2,1,0:T(8,128)(2,1)}), bf16[32,8,128]{2,1,0:T(8,128)(2,1)S(1)}, u32[]{:S(2)}, u32[]{:S(2)}) async-start(bf16[32,8,128]{2,1,0:T(8,128)(2,1)} %shard_map.133), calls=%async_computation.1 | async-start | bytes 131072 | tf_op jit(solution)/shard_map/all_to_all | solution.py:285
  59.7 0.1 constant_dynamic-slice_fusion
  59.8 3.3 %collective-permute-start.2 = (bf16[128,4,128]{2,1,0:T(4,128)(2,1)S(1)}, bf16[128,4,128]{2,1,0:T(4,128)(2,1)S(1)}, u32[]{:S(2)}, u32[]{:S(2)}) collective-permute-start(bf16[128,4,128]{2,1,0:T(4,128)(2,1)S(1)} %get-tuple-element.19), channel_id=1, source_target_pairs={{0,8},{8,0},{1,9},{9,1},{2,10},{10,2},{3,11},{11,3},{4,12},{12,4},... | collective-permute-start | bytes 393224 | tf_op jit(solution)/shard_map/ppermute | solution.py:274
  63.1 11.8 %all-to-all-done.1.in_ref = bf16[32,8,128]{2,1,0:T(8,128)(2,1)S(1)} async-done(((bf16[32,8,128]{2,1,0:T(8,128)(2,1)}), bf16[32,8,128]{2,1,0:T(8,128)(2,1)S(1)}, u32[]{:S(2)}, u32[]{:S(2)}) %all-to-all-start.1) | async-done | bytes 65568 | tf_op jit(solution)/shard_map/all_to_all | solution.py:285
  74.9 0.7 shard_map.134.after_ref.asked_ref
  75.6 4.7 %all-to-all-start.2 = ((f32[32,4,128]{2,1,0:T(4,128)}), f32[32,4,128]{2,1,0:T(4,128)S(1)}, u32[]{:S(2)}, u32[]{:S(2)}) async-start(f32[32,4,128]{2,1,0:T(4,128)} %shard_map.134.after_ref.asked_ref), calls=%async_computation.2 | async-start | bytes 131072 | tf_op jit(solution)/shard_map/all_to_all | solution.py:295
  80.3 0.1 pad_add_fusion.place_ref
  80.4 0.0 collective-permute-done.2.after_ref
  80.4 9.3 %all-gather.3.cloned.1.call-done = bf16[32,2,128,128]{3,2,1,0:T(8,128)(2,1)} async-done(((bf16[2,2,128,128]{3,2,1,0:T(8,128)(2,1)}), bf16[32,2,128,128]{3,2,1,0:T(8,128)(2,1)}) %all-gather.3.cloned.1.call-update) | async-done | bytes 2097168 | tf_op jit(solution)/shard_map/all_gather | solution.py:254
  89.7 1.6 %copy-done.10 = bf16[32,2,128,128]{3,2,1,0:T(8,128)(2,1)S(1)} copy-done((bf16[32,2,128,128]{3,2,1,0:T(8,128)(2,1)S(1)}, bf16[32,2,128,128]{3,2,1,0:T(8,128)(2,1)}, u32[]{:S(2)}) %copy-start.10) | copy-done | bytes 2097176
  91.2 1.7 %shard_map.135 = bf16[512,128]{1,0:T(8,128)(2,1)S(1)} custom-call(s32[3]{0:T(128)S(1)} %pad_add_fusion.place_ref, bf16[512,128]{1,0:T(8,128)(2,1)S(1)} %bitcast.50, bf16[8,2,2,2,128,128]{5,4,3,2,1,0:T(8,128)(2,1)S(1)} %bitcast.55, f32[32,4,128]{2,1,0:T(4,128)} %shard_map.134.after_ref.asked_ref), custom_call_target="tpu_custom_call" | custom-call | flops 1073741824 | bytes 16777216 | tf_op jit(solution)/shard_map/pallas_call | solution.py:22
  93.0 3.5 %collective-permute-start.3 = (bf16[128,4,128]{2,1,0:T(4,128)(2,1)S(1)}, bf16[128,4,128]{2,1,0:T(4,128)(2,1)S(1)}, u32[]{:S(2)}, u32[]{:S(2)}) collective-permute-start(bf16[128,4,128]{2,1,0:T(4,128)(2,1)S(1)} %bitcast.48), channel_id=1, source_target_pairs={{0,136},{8,128},{128,264},{136,256},{256,392},{264,384},{384,520},... | collective-permute-start | bytes 393224 | tf_op jit(solution)/shard_map/ppermute | solution.py:314
  96.5 1.1 shard_map.137.read_ref
  97.6 0.0 all-to-all-done.2.enter_ref
  97.6 3.4 %shard_map.138 = bf16[128,2048]{1,0:T(8,128)(2,1)S(1)} custom-call(f32[128,2048]{1,0:T(8,128)S(1)} %shard_map.132.step_ref, bf16[128,2048]{1,0:T(8,128)(2,1)S(1)} %get-tuple-element.14.after_ref.act_ref, f32[4,16,128]{2,1,0:T(8,128)S(1)} %all-to-all-done.maps_ref, bf16[128,256]{1,0:T(8,128)(2,1)S(1)} %shard_map.137.read_ref, f32[8,2048]{1,0:T(8,128)S(1)} %bitcast.46, ...), custom_call_target="tpu_custom_call" | custom-call | bytes 16777216 | tf_op jit(solution)/shard_map/pallas_call | solution.py:22
  101.0 3.7 %collective-permute-start.5 = (bf16[128,2048]{1,0:T(8,128)(2,1)S(1)}, bf16[128,2048]{1,0:T(8,128)(2,1)S(1)}, u32[]{:S(2)}, u32[]{:S(2)}) collective-permute-start(bf16[128,2048]{1,0:T(8,128)(2,1)S(1)} %shard_map.138), channel_id=1, source_target_pairs={{0,128},{128,256},{256,384},{384,512},{512,640},{640,768},{768,896... | collective-permute-start | bytes 1572872 | tf_op jit(solution)/shard_map/ppermute | solution.py:331
  104.6 0.0 collective-permute-done.3.after_ref
  104.7 0.0 copy-done.11
  104.7 1.4 %shard_map.136 = bf16[512,128]{1,0:T(8,128)(2,1)S(1)} custom-call(s32[3]{0:T(128)S(1)} %pad_add_fusion.place_ref, bf16[512,128]{1,0:T(8,128)(2,1)S(1)} %bitcast.51, bf16[8,2,2,2,128,128]{5,4,3,2,1,0:T(8,128)(2,1)S(1)} %bitcast.56, bf16[128,4,128]{2,1,0:T(4,128)(2,1)S(1)} %collective-permute-done.3.after_ref), custom_call_target="tpu_custom_call" | custom-call | flops 1073741824 | bytes 16777216 | tf_op jit(solution)/shard_map/pallas_call | solution.py:22
  106.0 2.7 %collective-permute-start.4 = (bf16[128,4,128]{2,1,0:T(4,128)(2,1)S(1)}, bf16[128,4,128]{2,1,0:T(4,128)(2,1)S(1)}, u32[]{:S(2)}, u32[]{:S(2)}) collective-permute-start(bf16[128,4,128]{2,1,0:T(4,128)(2,1)S(1)} %bitcast.57), channel_id=1, source_target_pairs={{0,128},{128,256},{256,384},{384,512},{512,640},{640,768},{768,896... | collective-permute-start | bytes 393224 | tf_op jit(solution)/shard_map/ppermute | solution.py:333
  108.7 11.1 %collective-permute-done.4 = bf16[128,4,128]{2,1,0:T(4,128)(2,1)S(1)} collective-permute-done((bf16[128,4,128]{2,1,0:T(4,128)(2,1)S(1)}, bf16[128,4,128]{2,1,0:T(4,128)(2,1)S(1)}, u32[]{:S(2)}, u32[]{:S(2)}) %collective-permute-start.4) | collective-permute-done | bytes 131104 | tf_op jit(solution)/shard_map/ppermute | solution.py:333
  119.9 0.8 maximum_bitcast_fusion
  120.7 0.0 collective-permute-done.5
  120.7 0.8 copy.33
  (17 shorter events, 0.1 us)
Async XLA Ops:
  7.2 32.4 %copy-start.4 = (bf16[1,128,512]{2,1,0:T(8,128)(2,1)S(1)}, bf16[1,128,512]{2,1,0:T(8,128)(2,1)}, u32[]{:S(2)}) copy-start(bf16[1,128,512]{2,1,0:T(8,128)(2,1)} %param.16) | copy-start | bytes 393220
  7.2 32.4 %copy-start.8 = (f32[1,2048]{1,0:T(1,128)S(1)}, f32[1,2048]{1,0:T(1,128)}, u32[]{:S(2)}) copy-start(f32[1,2048]{1,0:T(1,128)} %bias_ref.3) | copy-start | bytes 24580
  7.2 82.5 %all-gather.3.cloned.1.call-start = ((), (), s32[]{:S(2)}) async-start(), calls=%async_computation.3 | async-start | bytes 2228224 | tf_op jit(solution)/shard_map/all_gather | solution.py:254
  8.5 20.5 %collective-permute-start = (bf16[2,128,128]{2,1,0:T(8,128)(2,1)S(1)}, bf16[2,128,128]{2,1,0:T(8,128)(2,1)S(1)}, u32[]{:S(2)}, u32[]{:S(2)}) collective-permute-start(bf16[2,128,128]{2,1,0:T(8,128)(2,1)S(1)} %bitcast.64), channel_id=1, source_target_pairs={{0,8},{8,0},{1,9},{9,1},{2,10},{10,2},{3,11},{11,3},{4,12},{12,4},... | collective-permute-start | bytes 196616 | tf_op jit(solution)/shard_map/ppermute | solution.py:251
  14.2 16.1 %collective-permute-start.1 = (bf16[16,2048]{1,0:T(8,128)(2,1)S(1)}, bf16[16,2048]{1,0:T(8,128)(2,1)S(1)}, u32[]{:S(2)}, u32[]{:S(2)}) collective-permute-start(bf16[16,2048]{1,0:T(8,128)(2,1)S(1)} %slice_bitcast_fusion), channel_id=1, source_target_pairs={{0,4},{4,8},{8,12},{12,16},{16,20},{20,24},{24,28},{28,32},{32,36}... | collective-permute-start | bytes 196616 | tf_op jit(solution)/shard_map/ppermute | solution.py:252
  31.0 1.0 copy-start.1
  32.0 0.8 copy-start.5
  32.9 0.8 copy-start.6
  33.6 0.7 copy-start.7
  36.1 7.7 %copy-start.3 = (f32[1,8,2048]{2,1,0:T(8,128)S(1)}, f32[1,8,2048]{2,1,0:T(8,128)}, u32[]{:S(2)}) copy-start(f32[1,8,2048]{2,1,0:T(8,128)} %param.19) | copy-start | bytes 196612
  36.1 7.7 %all-to-all-start = ((f32[4,16,128]{2,1,0:T(8,128)}), f32[4,16,128]{2,1,0:T(8,128)S(1)}, u32[]{:S(2)}, u32[]{:S(2)}) async-start(f32[4,16,128]{2,1,0:T(8,128)} %get-tuple-element.10), calls=%async_computation | async-start | bytes 65536 | tf_op jit(solution)/shard_map/all_to_all | solution.py:270
  39.6 1.6 %copy-start = (bf16[1,512,2048]{2,1,0:T(8,128)(2,1)S(1)}, bf16[1,512,2048]{2,1,0:T(8,128)(2,1)}, u32[]{:S(2)}) copy-start(bf16[1,512,2048]{2,1,0:T(8,128)(2,1)} %param.17) | copy-start | bytes 6291460
  41.2 18.5 %copy-start.12 = (bf16[1,128,8,128]{3,2,1,0:T(8,128)(2,1)S(1)}, bf16[1,128,8,128]{3,2,1,0:T(8,128)(2,1)}, u32[]{:S(2)}) copy-start(bf16[1,128,8,128]{3,2,1,0:T(8,128)(2,1)} %param.12) | copy-start | bytes 786436
  47.8 27.1 %all-to-all-start.1 = ((bf16[32,8,128]{2,1,0:T(8,128)(2,1)}), bf16[32,8,128]{2,1,0:T(8,128)(2,1)S(1)}, u32[]{:S(2)}, u32[]{:S(2)}) async-start(bf16[32,8,128]{2,1,0:T(8,128)(2,1)} %shard_map.133), calls=%async_computation.1 | async-start | bytes 131072 | tf_op jit(solution)/shard_map/all_to_all | solution.py:285
  59.8 20.5 %collective-permute-start.2 = (bf16[128,4,128]{2,1,0:T(4,128)(2,1)S(1)}, bf16[128,4,128]{2,1,0:T(4,128)(2,1)S(1)}, u32[]{:S(2)}, u32[]{:S(2)}) collective-permute-start(bf16[128,4,128]{2,1,0:T(4,128)(2,1)S(1)} %get-tuple-element.19), channel_id=1, source_target_pairs={{0,8},{8,0},{1,9},{9,1},{2,10},{10,2},{3,11},{11,3},{4,12},{12,4},... | collective-permute-start | bytes 393224 | tf_op jit(solution)/shard_map/ppermute | solution.py:274
  75.6 22.0 %all-to-all-start.2 = ((f32[32,4,128]{2,1,0:T(4,128)}), f32[32,4,128]{2,1,0:T(4,128)S(1)}, u32[]{:S(2)}, u32[]{:S(2)}) async-start(f32[32,4,128]{2,1,0:T(4,128)} %shard_map.134.after_ref.asked_ref), calls=%async_computation.2 | async-start | bytes 131072 | tf_op jit(solution)/shard_map/all_to_all | solution.py:295
  89.7 1.6 %copy-start.10 = (bf16[32,2,128,128]{3,2,1,0:T(8,128)(2,1)S(1)}, bf16[32,2,128,128]{3,2,1,0:T(8,128)(2,1)}, u32[]{:S(2)}) copy-start(bf16[32,2,128,128]{3,2,1,0:T(8,128)(2,1)} %all-gather.3.cloned.1.call-done) | copy-start | bytes 6291460
  91.2 6.4 %copy-start.2 = (bf16[1,128,2048]{2,1,0:T(8,128)(2,1)S(1)}, bf16[1,128,2048]{2,1,0:T(8,128)(2,1)}, u32[]{:S(2)}) copy-start(bf16[1,128,2048]{2,1,0:T(8,128)(2,1)} %param.15) | copy-start | bytes 1572868
  91.2 6.4 %copy-start.9 = (f32[1,2048]{1,0:T(1,128)S(1)}, f32[1,2048]{1,0:T(1,128)}, u32[]{:S(2)}) copy-start(f32[1,2048]{1,0:T(1,128)} %skip_ref.1) | copy-start | bytes 24580
  93.0 11.7 %collective-permute-start.3 = (bf16[128,4,128]{2,1,0:T(4,128)(2,1)S(1)}, bf16[128,4,128]{2,1,0:T(4,128)(2,1)S(1)}, u32[]{:S(2)}, u32[]{:S(2)}) collective-permute-start(bf16[128,4,128]{2,1,0:T(4,128)(2,1)S(1)} %bitcast.48), channel_id=1, source_target_pairs={{0,136},{8,128},{128,264},{136,256},{256,392},{264,384},{384,520},... | collective-permute-start | bytes 393224 | tf_op jit(solution)/shard_map/ppermute | solution.py:314
  97.6 7.1 %copy-start.11 = (bf16[32,2,128,128]{3,2,1,0:T(8,128)(2,1)S(1)}, bf16[32,2,128,128]{3,2,1,0:T(8,128)(2,1)}, u32[]{:S(2)}) copy-start(bf16[32,2,128,128]{3,2,1,0:T(8,128)(2,1)} %all-gather.3.cloned.1.call-done) | copy-start | bytes 6291460
  101.0 19.7 %collective-permute-start.5 = (bf16[128,2048]{1,0:T(8,128)(2,1)S(1)}, bf16[128,2048]{1,0:T(8,128)(2,1)S(1)}, u32[]{:S(2)}, u32[]{:S(2)}) collective-permute-start(bf16[128,2048]{1,0:T(8,128)(2,1)S(1)} %shard_map.138), channel_id=1, source_target_pairs={{0,128},{128,256},{256,384},{384,512},{512,640},{640,768},{768,896... | collective-permute-start | bytes 1572872 | tf_op jit(solution)/shard_map/ppermute | solution.py:331
  106.0 13.8 %collective-permute-start.4 = (bf16[128,4,128]{2,1,0:T(4,128)(2,1)S(1)}, bf16[128,4,128]{2,1,0:T(4,128)(2,1)S(1)}, u32[]{:S(2)}, u32[]{:S(2)}) collective-permute-start(bf16[128,4,128]{2,1,0:T(4,128)(2,1)S(1)} %bitcast.57), channel_id=1, source_target_pairs={{0,128},{128,256},{256,384},{384,512},{512,640},{640,768},{768,896... | collective-permute-start | bytes 393224 | tf_op jit(solution)/shard_map/ppermute | solution.py:333
Sparse Core Ops, SparseCore 0:
  31.1 58.5 all-gather.2
